TPU v7x, 32 devices: a whole 2x2x4 slice. The times are simulated.
32 devices in a mesh: seq: 8 (over z, x), tp: 4 (over y, core).
Axes of the slice: x: 2, y: 2, z: 4, core: 2. Of those that a mesh axis runs over, the one named last changes fastest.
Arguments:
- tokens: bfloat16 [4, 4096, 768], P(None, 'seq'), may hold values from -6 to 6
- query_weight: bfloat16 [768, 768], P(None, 'tp'), may hold values from -0.21875 to 0.21875
- query_bias: bfloat16 [12, 64], P('tp'), may hold values from -4 to 4
- key_weight: bfloat16 [768, 768], P(None, 'tp'), may hold values from -0.21875 to 0.21875
- value_weight: bfloat16 [768, 768], P(None, 'tp'), may hold values from -0.21875 to 0.21875
- value_bias: bfloat16 [12, 64], P('tp'), may hold values from -4 to 4
- conv_weight: bfloat16 [12, 33], P('tp'), may hold values from -1 to 1
- output_weight: bfloat16 [768, 768], P('tp'), may hold values from -0.21875 to 0.21875
- output_bias: bfloat16 [768], replicated, may hold values from -3 to 3
- first_gain: bfloat16 [768], replicated, may hold values from 0.5 to 1.5
- first_shift: bfloat16 [768], replicated, may hold values from -3 to 3
- up_weight: bfloat16 [768, 3072], P(None, 'tp'), may hold values from -0.21875 to 0.21875
- up_bias: bfloat16 [3072], P('tp'), may hold values from -6 to 6
- down_weight: bfloat16 [3072, 768], P('tp'), may hold values from -0.109375 to 0.109375
- down_bias: bfloat16 [768], replicated, may hold values from -3 to 3
- second_gain: bfloat16 [768], replicated, may hold values from 0.5 to 1.5
- second_shift: bfloat16 [768], replicated, may hold values from -3 to 3
- segment_sizes: int32 [4, 8, 64], replicated, may hold values from 0 to 96, as said below
- cotangent: bfloat16 [4, 4096, 768], P(None, 'seq'), may hold values from -6 to 6
Outputs:
- layer_out: bfloat16 [4, 4096, 768], P(None, 'seq')
- grad_tokens: float32 [4, 4096, 768], P(None, 'seq')
- grad_query_weight: float32 [768, 768], P('seq', 'tp')
- grad_query_bias: float32 [12, 64], P('tp', 'seq')
- grad_key_weight: float32 [768, 768], P('seq', 'tp')
- grad_value_weight: float32 [768, 768], P('seq', 'tp')
- grad_value_bias: float32 [12, 64], P('tp')
- grad_conv_weight: float32 [12, 33], P('tp')
- grad_output_weight: float32 [768, 768], P('tp', 'seq')
- grad_output_bias: float32 [768], replicated
- grad_first_gain: float32 [768], replicated
- grad_first_shift: float32 [768], replicated
- grad_up_weight: float32 [768, 3072], P('seq', 'tp')
- grad_up_bias: float32 [3072], P('tp')
- grad_down_weight: float32 [3072, 768], P('tp', 'seq')
- grad_down_bias: float32 [768], replicated
- grad_second_gain: float32 [768], replicated
- grad_second_shift: float32 [768], replicated
Inputs may be any that keep to these rules, and one draw needn't show every extreme that they name: `segment_sizes`: row by row, the sizes of the 64 consecutive landmark segments of each of up to 8 items packed in order; a row's sizes add up to 4096; each item holds a multiple of 512 tokens and each of its segments at least one; unused item places come last and hold zeros; for every g below 1, some row r + g is one single item.
All inputs are finite; a program needn't handle non-finite values.
Results may differ from a plain program's by a relative error of at most 0.023.
Values may be sent and summed in bfloat16 or wider, within the bound.
No kernel may reach another device: no remote copies, remote signals or barrier semaphores. Data moves between devices by JAX's collectives and lax.ppermute only.
A program may use at most 192 MiB of HBM per device.

v0:
```python
import jax
import jax.numpy as jnp
from jax import lax
from jax.sharding import PartitionSpec as P

HEAD_DIM = 64
TAPS = 33
SWEEPS = 6
SPAN = 4096


highest = lax.Precision.HIGHEST
epsilon = 1e-05
very_negative = -1e30


def as_sent(shard):

    def short(part):
        return part.astype(jnp.bfloat16) if part.dtype == jnp.float32 else part

    return jax.tree.map(short, shard)


def swapped(shard, axis, distance):
    return lax.ppermute(shard, axis, [(i, i ^ 1 << distance) for i in range(lax.axis_size(axis))])


def extended(cells, sides, width):
    for axis, dim in sides:
        count = lax.axis_size(axis)
        ends = count - 1
        head = lax.slice_in_dim(cells, 0, width, axis=dim)
        tail = lax.slice_in_dim(cells, cells.shape[dim] - width, cells.shape[dim], axis=dim)
        cells = jnp.concatenate(
            [
                lax.ppermute(tail, axis, [(i, (i + 1) % count) for i in range(ends)]),
                cells,
                lax.ppermute(head, axis, [((i + 1) % count, i) for i in range(ends)]),
            ],
            axis=dim,
        )
    return cells


def count_below(ends, positions):
    return jnp.sum((ends[:, None, :] <= positions[:, :, None]).astype(jnp.int32), axis=2)


def newton_inverse(kernel):
    size = kernel.shape[-1]
    column_sums = jnp.sum(kernel, axis=-2)
    bound = jnp.sqrt(jnp.sum(column_sums * column_sums, axis=-1))[..., None, None]
    identity = jnp.eye(size, dtype=kernel.dtype)
    inverse = jnp.swapaxes(kernel, -1, -2) / bound
    for sweep in range(SWEEPS):
        product = jnp.matmul(kernel, inverse, precision=highest)
        inner = 7.0 * identity - product
        inner = 15.0 * identity - jnp.matmul(product, inner, precision=highest)
        inner = 13.0 * identity - jnp.matmul(product, inner, precision=highest)
        inverse = 0.25 * jnp.matmul(inverse, inner, precision=highest)
    return inverse


def landmark_core(land_query, land_key, mixed_values):
    scores = jnp.einsum("rmhd,rnhd->rhmn", land_query, land_key, precision=highest)
    powers = jnp.exp(scores - jnp.max(scores, axis=-1, keepdims=True))
    kernel = powers / jnp.sum(powers, axis=-1, keepdims=True)
    return jnp.einsum("rhmn,rhnd->rhmd", newton_inverse(kernel), mixed_values, precision=highest)


def layer_norm(values, gain, shift):
    centred = values - jnp.mean(values, axis=-1, keepdims=True)
    inverse = lax.rsqrt(jnp.mean(centred * centred, axis=-1, keepdims=True) + epsilon)
    normed = centred * inverse
    return (normed * gain + shift, normed, inverse)


def norm_back(upstream, gain, normed, inverse):
    scaled = upstream * gain
    centred = scaled - jnp.mean(scaled, axis=-1, keepdims=True)
    return (centred - normed * jnp.mean(scaled * normed, axis=-1, keepdims=True)) * inverse


def gelu(values):
    return 0.5 * values * (1.0 + lax.erf(values * 0.7071067811865476))


def add_parts(first, second):
    return jax.tree.map(jnp.add, first, second)


def butterfly(value, levels, swapper, combine):
    for level in range(levels):
        value = combine(value, swapper(value, level))
    return value


def swap_landmarks(value, level):
    return jax.tree.map(
        lambda part, own: part.astype(own.dtype), swapped(as_sent(value), "seq", level), value
    )


def swap_context(value, level):
    return swapped(value.astype(jnp.bfloat16), "seq", level).astype(value.dtype)


def swap_dots(value, level):
    return swapped(value, "seq", level)


def swap_land_back(value, level):
    return jax.tree.map(
        lambda part, own: part.astype(own.dtype), swapped(as_sent(value), "seq", level), value
    )


def per_device(
    tokens,
    query_weight,
    query_bias,
    key_weight,
    value_weight,
    value_bias,
    conv_weight,
    output_weight,
    output_bias,
    first_gain,
    first_shift,
    up_weight,
    up_bias,
    down_weight,
    down_bias,
    second_gain,
    second_shift,
    segment_sizes,
    cotangent,
):
    rows, width, model = tokens.shape
    channels = query_weight.shape[1]
    heads = channels // HEAD_DIM
    items = segment_sizes.shape[1]
    marks = segment_sizes.shape[2]
    reach = TAPS // 2
    scale = HEAD_DIM ** (-0.25)
    total = rows * width
    group = SPAN // width
    levels = group.bit_length() - 1
    device = lax.axis_index("seq")
    local_index = device % group
    group_number = device // group
    span = SPAN
    start = local_index * width
    all_sizes = segment_sizes.reshape(rows, segment_sizes.shape[0] // rows, items, marks)
    row_sizes = lax.dynamic_index_in_dim(all_sizes, group_number, axis=1, keepdims=False)
    sizes_flat = row_sizes.reshape(rows, items * marks)
    item_ends = jnp.cumsum(jnp.sum(row_sizes, axis=2), axis=1)
    local_pos = jnp.broadcast_to(start + jnp.arange(width, dtype=jnp.int32)[None, :], (rows, width))
    token_slot = count_below(jnp.cumsum(sizes_flat, axis=1), local_pos)
    own_item = token_slot[:, 0] // marks
    token_mark = token_slot - own_item[:, None] * marks
    own_sizes = jnp.take_along_axis(row_sizes, own_item[:, None, None], axis=1)[:, 0, :]
    own_count = jnp.maximum(own_sizes, 1).astype(jnp.float32)[:, :, None]
    member = token_mark[:, :, None] == jnp.arange(marks, dtype=jnp.int32)[None, None, :]
    item_hot = (own_item[:, None] == jnp.arange(items, dtype=jnp.int32)[None, :]).astype(
        jnp.float32
    )

    def item_mask(ndim, axis):
        shape = [1] * ndim
        shape[0] = rows
        shape[axis] = items
        return item_hot.reshape(shape)

    def spread(part, axis):
        grown = item_mask(part.ndim + 1, axis) * jnp.expand_dims(part, axis)
        return grown.reshape(part.shape[:axis] + (items * marks,) + part.shape[axis + 1 :])

    def pick(table, axis):
        split_table = table.reshape(table.shape[:axis] + (items, marks) + table.shape[axis + 1 :])
        return jnp.sum(item_mask(table.ndim + 1, axis) * split_table, axis=axis)

    def split_heads(array, length):
        return array.reshape(rows, length, heads, HEAD_DIM)

    flat = tokens.reshape(total, model)
    query = (
        scale
        * (
            jnp.dot(flat, query_weight, preferred_element_type=jnp.float32)
            + query_bias.reshape(-1).astype(jnp.float32)
        )
    ).astype(jnp.bfloat16)
    keys = (scale * jnp.dot(flat, key_weight, preferred_element_type=jnp.float32)).astype(
        jnp.bfloat16
    )
    values = (
        jnp.dot(flat, value_weight, preferred_element_type=jnp.float32)
        + value_bias.reshape(-1).astype(jnp.float32)
    ).astype(jnp.bfloat16)
    query_rows = query.reshape(rows, width, channels)
    key_rows = keys.reshape(rows, width, channels)
    value_rows = values.reshape(rows, width, channels)
    member_low = member.astype(jnp.bfloat16)
    part_query = jnp.einsum(
        "rtm,rtc->rmc", member_low, query_rows, preferred_element_type=jnp.float32
    )
    part_key = jnp.einsum("rtm,rtc->rmc", member_low, key_rows, preferred_element_type=jnp.float32)
    sum_query, sum_key = butterfly(
        (spread(part_query, 1), spread(part_key, 1)), levels, swap_landmarks, add_parts
    )
    land_query = (pick(sum_query, 1) / own_count).astype(jnp.bfloat16)
    land_key = (pick(sum_key, 1) / own_count).astype(jnp.bfloat16)
    query_heads = split_heads(query_rows, width)
    key_heads = split_heads(key_rows, width)
    value_heads = split_heads(value_rows, width)
    land_query_heads = split_heads(land_query, marks)
    land_key_heads = split_heads(land_key, marks)
    token_scores = jnp.einsum(
        "rthd,rmhd->rhtm", query_heads, land_key_heads, preferred_element_type=jnp.float32
    )
    token_powers = jnp.exp(token_scores - jnp.max(token_scores, axis=-1, keepdims=True))
    token_weights = token_powers / jnp.sum(token_powers, axis=-1, keepdims=True)
    token_low = token_weights.astype(jnp.bfloat16)
    key_scores = jnp.einsum(
        "rmhd,rthd->rhmt", land_query_heads, key_heads, preferred_element_type=jnp.float32
    )
    whole_keys = key_rows
    whole_values = value_rows
    for level in range(levels):
        far_keys, far_values = swapped((whole_keys, whole_values), "seq", level)
        lower_half = local_index // (1 << level) % 2 == 0
        whole_keys = jnp.where(
            lower_half,
            jnp.concatenate((whole_keys, far_keys), axis=1),
            jnp.concatenate((far_keys, whole_keys), axis=1),
        )
        whole_values = jnp.where(
            lower_half,
            jnp.concatenate((whole_values, far_values), axis=1),
            jnp.concatenate((far_values, whole_values), axis=1),
        )
    row_pos = jnp.broadcast_to(jnp.arange(span, dtype=jnp.int32)[None, :], (rows, span))
    valid = (count_below(item_ends, row_pos) == own_item[:, None])[:, None, None, :]
    scores = jnp.einsum(
        "rmhd,rphd->rhmp",
        land_query_heads,
        split_heads(whole_keys, span),
        preferred_element_type=jnp.float32,
    )
    key_max = jnp.max(jnp.where(valid, scores, very_negative), axis=-1)
    powers = jnp.exp(jnp.where(valid, scores - key_max[..., None], very_negative))
    key_total = jnp.sum(powers, axis=-1)
    mixed_values = jnp.einsum(
        "rhmp,rphd->rhmd",
        (powers / key_total[..., None]).astype(jnp.bfloat16),
        split_heads(whole_values, span),
        preferred_element_type=jnp.float32,
    )
    mixed_land, core_back = jax.vjp(
        landmark_core,
        land_query_heads.astype(jnp.float32),
        land_key_heads.astype(jnp.float32),
        mixed_values,
    )
    mixed_low = mixed_land.astype(jnp.bfloat16)
    nystrom = jnp.einsum(
        "rhtm,rhmd->rthd", token_low, mixed_low, preferred_element_type=jnp.float32
    )
    value_rim = extended(value_rows, (("seq", 1),), reach)
    rim_pos = start - reach + jnp.arange(width + 2 * reach, dtype=jnp.int32)
    rim_inside = (rim_pos >= 0) & (rim_pos < span)
    rim_item = count_below(
        item_ends,
        jnp.broadcast_to(jnp.clip(rim_pos, 0, span - 1)[None, :], (rows, width + 2 * reach)),
    )
    rim_keep = (rim_inside[None, :] & (rim_item == own_item[:, None]))[:, :, None]
    kept_values = jnp.where(rim_keep, value_rim.astype(jnp.float32), 0.0).reshape(
        rows, width + 2 * reach, heads, HEAD_DIM
    )
    taps = conv_weight.astype(jnp.float32)
    convolved = jnp.zeros((rows, width, heads, HEAD_DIM), jnp.float32)
    for offset in range(TAPS):
        convolved = (
            convolved
            + kept_values[:, offset : offset + width] * taps[:, offset][None, None, :, None]
        )
    context = (nystrom + convolved).reshape(total, channels).astype(jnp.bfloat16)
    attention = lax.psum(
        jnp.dot(context, output_weight, preferred_element_type=jnp.float32).astype(jnp.bfloat16),
        "tp",
    ).astype(jnp.float32) + output_bias.astype(jnp.float32)
    first_gain32 = first_gain.astype(jnp.float32)
    second_gain32 = second_gain.astype(jnp.float32)
    first_out, first_normed, first_inverse = layer_norm(
        flat.astype(jnp.float32) + attention, first_gain32, first_shift.astype(jnp.float32)
    )
    first_low = first_out.astype(jnp.bfloat16)
    hidden = jnp.dot(first_low, up_weight, preferred_element_type=jnp.float32) + up_bias.astype(
        jnp.float32
    )
    active_low = gelu(hidden).astype(jnp.bfloat16)
    feed = lax.psum(
        jnp.dot(active_low, down_weight, preferred_element_type=jnp.float32).astype(jnp.bfloat16),
        "tp",
    ).astype(jnp.float32) + down_bias.astype(jnp.float32)
    layer_out, second_normed, second_inverse = layer_norm(
        first_out + feed, second_gain32, second_shift.astype(jnp.float32)
    )
    upstream = cotangent.reshape(total, model).astype(jnp.float32)
    grad_second_gain = jnp.sum(upstream * second_normed, axis=0)
    grad_second_shift = jnp.sum(upstream, axis=0)
    back_second = norm_back(upstream, second_gain32, second_normed, second_inverse)
    back_feed = back_second.astype(jnp.bfloat16)
    grad_down_bias = jnp.sum(back_feed.astype(jnp.float32), axis=0)
    grad_down_weight = jnp.einsum(
        "tf,td->fd", active_low, back_feed, preferred_element_type=jnp.float32
    )
    back_active = jnp.einsum(
        "td,fd->tf", back_feed, down_weight, preferred_element_type=jnp.float32
    )
    back_hidden = jax.vjp(gelu, hidden)[1](back_active)[0].astype(jnp.bfloat16)
    grad_up_bias = jnp.sum(back_hidden.astype(jnp.float32), axis=0)
    grad_up_weight = jnp.einsum(
        "td,tf->df", first_low, back_hidden, preferred_element_type=jnp.float32
    )
    back_first = back_second + lax.psum(
        jnp.einsum("tf,df->td", back_hidden, up_weight, preferred_element_type=jnp.float32).astype(
            jnp.bfloat16
        ),
        "tp",
    ).astype(jnp.float32)
    grad_first_gain = jnp.sum(back_first * first_normed, axis=0)
    grad_first_shift = jnp.sum(back_first, axis=0)
    back_input = norm_back(back_first, first_gain32, first_normed, first_inverse)
    back_attention = back_input.astype(jnp.bfloat16)
    grad_output_bias = jnp.sum(back_attention.astype(jnp.float32), axis=0)
    grad_output_weight = jnp.einsum(
        "tc,td->cd", context, back_attention, preferred_element_type=jnp.float32
    )
    back_context = jnp.einsum(
        "td,cd->tc", back_attention, output_weight, preferred_element_type=jnp.float32
    ).astype(jnp.bfloat16)
    back_context_rows = back_context.reshape(rows, width, channels)
    context_rim = extended(back_context_rows, (("seq", 1),), reach)
    kept_back = jnp.where(rim_keep, context_rim.astype(jnp.float32), 0.0).reshape(
        rows, width + 2 * reach, heads, HEAD_DIM
    )
    back_heads_wide = back_context_rows.astype(jnp.float32).reshape(rows, width, heads, HEAD_DIM)
    conv_values = jnp.zeros((rows, width, heads, HEAD_DIM), jnp.float32)
    tap_terms = []
    for offset in range(TAPS):
        lower = 2 * reach - offset
        conv_values = (
            conv_values + kept_back[:, lower : lower + width] * taps[:, offset][None, None, :, None]
        )
        tap_terms.append(
            jnp.sum(back_heads_wide * kept_values[:, offset : offset + width], axis=(0, 1, 3))
        )
    conv_part = jnp.stack(tap_terms, axis=1)
    back_heads = split_heads(back_context_rows, width)
    part_mixed = jnp.einsum(
        "rhtm,rthd->rhmd", token_low, back_heads, preferred_element_type=jnp.float32
    )
    back_mixed_land = pick(butterfly(spread(part_mixed, 2), levels, swap_context, add_parts), 2)
    back_token = jnp.einsum(
        "rthd,rhmd->rhtm", back_heads, mixed_low, preferred_element_type=jnp.float32
    )
    back_token_scores = (
        token_weights * (back_token - jnp.sum(token_weights * back_token, axis=-1, keepdims=True))
    ).astype(jnp.bfloat16)
    back_query_token = jnp.einsum(
        "rhtm,rmhd->rthd", back_token_scores, land_key_heads, preferred_element_type=jnp.float32
    )
    part_land_key = jnp.einsum(
        "rhtm,rthd->rmhd", back_token_scores, query_heads, preferred_element_type=jnp.float32
    )
    back_land_query_a, back_land_key_a, back_mixed = core_back(back_mixed_land)
    back_mixed_low = back_mixed.astype(jnp.bfloat16)
    key_weights = jnp.exp(key_scores - key_max[..., None]) / key_total[..., None]
    back_key_weights = jnp.einsum(
        "rhmd,rthd->rhmt", back_mixed_low, value_heads, preferred_element_type=jnp.float32
    )
    key_dots = pick(
        butterfly(
            spread(jnp.sum(key_weights * back_key_weights, axis=-1), 2),
            levels,
            swap_dots,
            add_parts,
        ),
        2,
    )
    back_key_scores = (key_weights * (back_key_weights - key_dots[..., None])).astype(jnp.bfloat16)
    part_land_query = jnp.einsum(
        "rhmt,rthd->rmhd", back_key_scores, key_heads, preferred_element_type=jnp.float32
    )
    back_key_direct = jnp.einsum(
        "rhmt,rmhd->rthd", back_key_scores, land_query_heads, preferred_element_type=jnp.float32
    )
    back_value_direct = jnp.einsum(
        "rhmt,rhmd->rthd",
        key_weights.astype(jnp.bfloat16),
        back_mixed_low,
        preferred_element_type=jnp.float32,
    )
    back_values = (back_value_direct + conv_values).reshape(total, channels).astype(jnp.bfloat16)
    value_bias_part = jnp.sum(back_values.astype(jnp.float32), axis=0).reshape(heads, HEAD_DIM)
    sum_land_query, sum_land_key = butterfly(
        (
            spread(part_land_query.reshape(rows, marks, channels), 1),
            spread(part_land_key.reshape(rows, marks, channels), 1),
        ),
        levels,
        swap_land_back,
        add_parts,
    )
    (
        grad_conv_weight,
        grad_value_bias,
        grad_up_bias,
        grad_output_bias,
        grad_down_bias,
        grad_first_gain,
        grad_first_shift,
        grad_second_gain,
        grad_second_shift,
    ) = lax.psum(
        (
            conv_part,
            value_bias_part,
            grad_up_bias,
            grad_output_bias,
            grad_down_bias,
            grad_first_gain,
            grad_first_shift,
            grad_second_gain,
            grad_second_shift,
        ),
        "seq",
    )
    back_land_query = pick(sum_land_query, 1) + back_land_query_a.reshape(rows, marks, channels)
    back_land_key = pick(sum_land_key, 1) + back_land_key_a.reshape(rows, marks, channels)
    member_wide = member.astype(jnp.float32)
    back_query = (
        (
            back_query_token.reshape(rows, width, channels)
            + jnp.einsum(
                "rtm,rmc->rtc", member_wide, back_land_query / own_count, precision=highest
            )
        )
        .reshape(total, channels)
        .astype(jnp.bfloat16)
    )
    back_keys = (
        (
            back_key_direct.reshape(rows, width, channels)
            + jnp.einsum("rtm,rmc->rtc", member_wide, back_land_key / own_count, precision=highest)
        )
        .reshape(total, channels)
        .astype(jnp.bfloat16)
    )
    query_weight_part = scale * jnp.einsum(
        "td,tc->dc", flat, back_query, preferred_element_type=jnp.float32
    )
    key_weight_part = scale * jnp.einsum(
        "td,tc->dc", flat, back_keys, preferred_element_type=jnp.float32
    )
    value_weight_part = jnp.einsum(
        "td,tc->dc", flat, back_values, preferred_element_type=jnp.float32
    )
    query_bias_part = scale * jnp.sum(back_query.astype(jnp.float32), axis=0).reshape(
        heads, HEAD_DIM
    )
    projected = scale * (
        jnp.einsum("tc,dc->td", back_query, query_weight, preferred_element_type=jnp.float32)
        + jnp.einsum("tc,dc->td", back_keys, key_weight, preferred_element_type=jnp.float32)
    ) + jnp.einsum("tc,dc->td", back_values, value_weight, preferred_element_type=jnp.float32)
    grad_tokens = back_input + lax.psum(projected.astype(jnp.bfloat16), "tp").astype(jnp.float32)
    (
        grad_query_weight,
        grad_key_weight,
        grad_value_weight,
        grad_output_weight,
        grad_up_weight,
        grad_down_weight,
        grad_query_bias,
    ) = (
        lax.psum_scatter(query_weight_part, "seq", scatter_dimension=0, tiled=True),
        lax.psum_scatter(key_weight_part, "seq", scatter_dimension=0, tiled=True),
        lax.psum_scatter(value_weight_part, "seq", scatter_dimension=0, tiled=True),
        lax.psum_scatter(grad_output_weight, "seq", scatter_dimension=1, tiled=True),
        lax.psum_scatter(grad_up_weight, "seq", scatter_dimension=0, tiled=True),
        lax.psum_scatter(grad_down_weight, "seq", scatter_dimension=1, tiled=True),
        lax.psum_scatter(query_bias_part, "seq", scatter_dimension=1, tiled=True),
    )
    return (
        layer_out.reshape(rows, width, model).astype(jnp.bfloat16),
        grad_tokens.reshape(rows, width, model),
        grad_query_weight,
        grad_query_bias,
        grad_key_weight,
        grad_value_weight,
        grad_value_bias,
        grad_conv_weight,
        grad_output_weight,
        grad_output_bias,
        grad_first_gain,
        grad_first_shift,
        grad_up_weight,
        grad_up_bias,
        grad_down_weight,
        grad_down_bias,
        grad_second_gain,
        grad_second_shift,
    )


def solution(mesh):
    placed = (
        P(None, "seq", None),
        P(None, "tp"),
        P("tp", None),
        P(None, "tp"),
        P(None, "tp"),
        P("tp", None),
        P("tp", None),
        P("tp", None),
        P(),
        P(),
        P(),
        P(None, "tp"),
        P("tp"),
        P("tp", None),
        P(),
        P(),
        P(),
        P(),
        P(None, "seq", None),
    )
    return jax.shard_map(
        per_device,
        mesh=mesh,
        in_specs=placed,
        out_specs=(
            P(None, "seq", None),
            P(None, "seq", None),
            P("seq", "tp"),
            P("tp", "seq"),
            P("seq", "tp"),
            P("seq", "tp"),
            P("tp", None),
            P("tp", None),
            P("tp", "seq"),
            P(),
            P(),
            P(),
            P("seq", "tp"),
            P("tp"),
            P("tp", "seq"),
            P(),
            P(),
            P(),
        ),
        check_vma=False,
    )
```

profile of v0, /device:TPU:0, one launch (start us, length us, event | category | flops | bytes accessed | tf_op | source)
XLA Modules:
  0.0 1490.4 jit_solution(497281762094773589)
XLA Ops:
  54.3 17.5 %collective-permute-done = bf16[4,512,192]{1,2,0:T(8,128)(2,1)S(1)} collective-permute-done((bf16[4,512,192]{1,2,0:T(8,128)(2,1)}, bf16[4,512,192]{1,2,0:T(8,128)(2,1)S(1)}, u32[]{:S(2)}, u32[]{:S(2)}) %collective-permute-start) | collective-permute-done | bytes 786464 | tf_op jit(solution)/shard_map/ppermute | solution.py:26
  85.4 4.0 maximum_select_fusion.9
  89.4 3.9 collective-permute-done.1
  125.4 18.6 %collective-permute-done.7 = bf16[4,1024,192]{1,0,2:T(4,128)(2,1)} collective-permute-done((bf16[4,1024,192]{1,0,2:T(4,128)(2,1)}, bf16[4,1024,192]{1,0,2:T(4,128)(2,1)}, u32[]{:S(2)}, u32[]{:S(2)}) %collective-permute-start.7) | collective-permute-done | bytes 1572896 | tf_op jit(solution)/shard_map/ppermute | solution.py:26
  143.9 6.9 maximum_select_fusion.5
  153.2 24.3 %collective-permute-done.2 = bf16[4,512,192]{1,2,0:T(8,128)(2,1)S(1)} collective-permute-done((bf16[4,512,192]{1,2,0:T(8,128)(2,1)S(1)}, bf16[4,512,192]{1,2,0:T(8,128)(2,1)S(1)}, u32[]{:S(2)}, u32[]{:S(2)}) %collective-permute-start.2) | collective-permute-done | bytes 786464 | tf_op jit(solution)/shard_map/ppermute | solution.py:26
  177.5 42.0 %collective-permute-done.4 = bf16[4,512,192]{1,2,0:T(8,128)(2,1)S(1)} collective-permute-done((bf16[4,512,192]{1,2,0:T(8,128)(2,1)S(1)}, bf16[4,512,192]{1,2,0:T(8,128)(2,1)S(1)}, u32[]{:S(2)}, u32[]{:S(2)}) %collective-permute-start.4) | collective-permute-done | bytes 786464 | tf_op jit(solution)/shard_map/ppermute | solution.py:26
  219.5 4.0 convert_add_fusion.14
  239.9 168.6 %collective-permute-done.5 = bf16[4,512,192]{1,2,0:T(8,128)(2,1)} collective-permute-done((bf16[4,512,192]{1,2,0:T(8,128)(2,1)}, bf16[4,512,192]{1,2,0:T(8,128)(2,1)}, u32[]{:S(2)}, u32[]{:S(2)}) %collective-permute-start.5) | collective-permute-done | bytes 786464 | tf_op jit(solution)/shard_map/ppermute | solution.py:26
  448.7 5.4 copy.859
  454.1 6.1 select_reduce_fusion
  464.6 6.2 collective-permute-done.11
  475.0 7.5 fusion.8
  483.4 14.0 fusion.100
  502.6 68.1 %all-reduce.7.cloned.1.call-done = bf16[2048,768]{1,0:T(8,128)(2,1)} async-done(((bf16[2048,768]{1,0:T(8,128)(2,1)}), bf16[2048,768]{1,0:T(8,128)(2,1)}) %all-reduce.7.cloned.1.call-update) | async-done | bytes 3145744 | tf_op jit(solution)/shard_map/psum | solution.py:290
  570.7 4.1 fusion.25
  578.9 5.0 multiply_convert_fusion
  585.5 3.9 convolution_convert_fusion.1
  590.2 4.0 convert_reduce_fusion
  594.2 64.0 %all-reduce.9.cloned.1.call-done = bf16[2048,768]{1,0:T(8,128)(2,1)} async-done(((bf16[2048,768]{1,0:T(8,128)(2,1)}), bf16[2048,768]{1,0:T(8,128)(2,1)}) %all-reduce.9.cloned.1.call-update) | async-done | bytes 3145744 | tf_op jit(solution)/shard_map/psum | solution.py:304
  658.2 5.1 fusion.234
  668.4 3.9 fusion.17
  672.3 6.0 convert_reduce_fusion.2
  680.0 4.0 convolution_convert_fusion
  684.1 68.6 %all-reduce.11.cloned.1.call-done = bf16[2048,768]{1,0:T(8,128)(2,1)} async-done(((bf16[2048,768]{1,0:T(8,128)(2,1)}), bf16[2048,768]{1,0:T(8,128)(2,1)}) %all-reduce.11.cloned.1.call-update) | async-done | bytes 3145744 | tf_op jit(solution)/shard_map/psum | solution.py:328
  752.7 9.4 multiply_reduce_fusion
  762.1 6.2 convert_reduce_fusion.3
  787.6 12.3 collective-permute-done.14
  813.7 9.3 collective-permute-done.15
  837.9 27.2 %collective-permute-done.16 = bf16[4,3,512,64]{2,3,1,0:T(8,128)(2,1)} collective-permute-done((bf16[4,3,512,64]{2,3,1,0:T(8,128)(2,1)}, bf16[4,3,512,64]{2,3,1,0:T(8,128)(2,1)}, u32[]{:S(2)}, u32[]{:S(2)}) %collective-permute-start.16) | collective-permute-done | bytes 786464 | tf_op jit(solution)/shard_map/ppermute | solution.py:26
  942.8 12.4 collective-permute-done.20
  959.4 12.1 collective-permute-done.21
  977.2 9.9 collective-permute-done.23
  989.8 16.3 %convert_reduce_fusion.5 = (f32[3,64]{1,0:T(4,128)}, bf16[4,512,3,64]{1,3,2,0:T(8,128)(2,1)}) fusion(f32[3]{0:T(128)S(1)} %copy-done.216, f32[4,544,3,64]{1,3,2,0:T(8,128)S(1)} %copy-done.116, f32[3]{0:T(128)S(1)} %copy-done.218, f32[3]{0:T(128)S(1)} %copy-done.220, f32[3]{0:T(128)S(1)} %copy-done.222, f32[3]{0:T(128)S(1)} %copy-done.224, ...), kind=kOutput, calls=%fused_computation.224 | convolution fusion | flops 77856576 | bytes 54363276 | tf_op jit(solution)/shard_map/rhmt,rhmd->rthd/dot_general | solution.py:401
  1007.4 10.7 collective-permute-done.24
  1018.1 3.8 convert_add_fusion.5
  1036.8 18.4 %collective-permute-done.25 = bf16[4,512,192]{1,2,0:T(8,128)(2,1)} collective-permute-done((bf16[4,512,192]{1,2,0:T(8,128)(2,1)}, bf16[4,512,192]{1,2,0:T(8,128)(2,1)}, u32[]{:S(2)}, u32[]{:S(2)}) %collective-permute-start.25) | collective-permute-done | bytes 786464 | tf_op jit(solution)/shard_map/ppermute | solution.py:26
  1072.9 7.8 fusion.204
  1080.8 7.9 fusion.124
  1100.3 7.8 fusion.63
  1109.7 6.0 fusion.45
  1123.5 35.1 %all-reduce.1 = (f32[3,64]{1,0:T(4,128)S(1)}, f32[3,64]{1,0:T(4,128)}, f32[3,33]{1,0:T(4,128)}, f32[768]{0:T(1024)}, f32[768]{0:T(1024)}, /*index=5*/f32[768]{0:...) all-reduce(f32[3,64]{1,0:T(4,128)S(1)} %mul.1334, ...), channel_id=3, replica_groups=mesh['seq'=8,'tp'=4] {'seq'}, use_global_device_ids=true, to_apply=%region_41.42.clone | all-reduce | flops 5859 | bytes 46872
  1159.3 7.2 convert_add_fusion
  1166.5 47.4 %reduce-scatter.18.cloned.1.call-done = f32[768,96]{0,1:T(8,128)} async-done(((f32[768,768]{0,1:T(8,128)}), f32[768,96]{0,1:T(8,128)}) %reduce-scatter.18.cloned.1.call-update) | async-done | bytes 294928 | tf_op jit(solution)/shard_map/reduce_scatter | solution.py:494
  1213.8 72.6 %reduce-scatter.16.cloned.1.call-done = f32[96,768]{1,0:T(8,128)} async-done(((f32[768,768]{1,0:T(8,128)}), f32[96,768]{1,0:T(8,128)}) %reduce-scatter.16.cloned.1.call-update) | async-done | bytes 294928 | tf_op jit(solution)/shard_map/reduce_scatter | solution.py:493
  1286.5 65.9 %reduce-scatter.24.cloned.1.call-done = f32[96,192]{1,0:T(8,128)} async-done(((f32[768,192]{1,0:T(8,128)}), f32[96,192]{1,0:T(8,128)}) %reduce-scatter.24.cloned.1.call-update) | async-done | bytes 73744
  1352.3 65.4 %reduce-scatter.22.cloned.1.call-done = f32[96,192]{1,0:T(8,128)} async-done(((f32[768,192]{1,0:T(8,128)}), f32[96,192]{1,0:T(8,128)}) %reduce-scatter.22.cloned.1.call-update) | async-done | bytes 73744
  1417.8 65.5 %reduce-scatter.20.cloned.1.call-done = f32[96,192]{1,0:T(8,128)} async-done(((f32[768,192]{1,0:T(8,128)}), f32[96,192]{1,0:T(8,128)}) %reduce-scatter.20.cloned.1.call-update) | async-done | bytes 73744
  (942 shorter events, 368.8 us)
Async XLA Ops:
  7.2 571.7 %copy-start = (bf16[768,768]{1,0:T(8,128)(2,1)S(1)}, bf16[768,768]{1,0:T(8,128)(2,1)}, u32[]{:S(2)}) copy-start(bf16[768,768]{1,0:T(8,128)(2,1)} %param.30) | copy-start | bytes 3538948
  7.2 563.5 %all-reduce.7.cloned.1.call-start = ((), (), s32[]{:S(2)}) async-start(), calls=%async_computation.6 | async-start | bytes 6291456 | tf_op jit(solution)/shard_map/psum | solution.py:290
  12.7 98.4 %collective-permute-start.9 = (bf16[4,512,192]{1,0,2:T(4,128)(2,1)}, bf16[4,512,192]{1,0,2:T(4,128)(2,1)}, u32[]{:S(2)}, u32[]{:S(2)}) collective-permute-start(bf16[4,512,192]{1,0,2:T(4,128)(2,1)} %reshape.643), channel_id=1, source_target_pairs={{0,4},{4,0},{8,12},{12,8},{16,20},{20,16},{24,28},{28,24},{1,5},{5... | collective-permute-start | bytes 2359304 | tf_op jit(solution)/shard_map/ppermute | solution.py:26
  20.2 65.2 %collective-permute-start.6 = (bf16[4,512,192]{1,0,2:T(4,128)(2,1)}, bf16[4,512,192]{1,0,2:T(4,128)(2,1)}, u32[]{:S(2)}, u32[]{:S(2)}) collective-permute-start(bf16[4,512,192]{1,0,2:T(4,128)(2,1)} %reshape.641), channel_id=1, source_target_pairs={{0,4},{4,0},{8,12},{12,8},{16,20},{20,16},{24,28},{28,24},{1,5},{5... | collective-permute-start | bytes 2359304 | tf_op jit(solution)/shard_map/ppermute | solution.py:26
  30.5 62.9 %copy-start.8 = (f32[4,512,192]{1,2,0:T(8,128)}, f32[4,512,192]{1,2,0:T(8,128)S(1)}, u32[]{:S(2)}) copy-start(f32[4,512,192]{1,2,0:T(8,128)S(1)} %copy.838) | copy-start | bytes 4718596
  32.3 39.5 %collective-permute-start = (bf16[4,512,192]{1,2,0:T(8,128)(2,1)}, bf16[4,512,192]{1,2,0:T(8,128)(2,1)S(1)}, u32[]{:S(2)}, u32[]{:S(2)}) collective-permute-start(bf16[4,512,192]{1,2,0:T(8,128)(2,1)} %multiply_convert_fusion.7), channel_id=1, source_target_pairs={{0,4},{4,0},{8,12},{12,8},{16,20},{20,16},{24,28},{28,24},{1,5},{5... | collective-permute-start | bytes 2359304 | tf_op jit(solution)/shard_map/ppermute | solution.py:26
  36.3 71.1 %collective-permute-start.12 = (bf16[4,16,192]{1,0,2:T(4,128)(2,1)}, bf16[4,16,192]{1,0,2:T(4,128)(2,1)}, u32[]{:S(2)}, u32[]{:S(2)}) collective-permute-start(bf16[4,16,192]{1,0,2:T(4,128)(2,1)} %get-tuple-element.267), channel_id=1, source_target_pairs={{0,4},{4,8},{8,12},{12,16},{16,20},{20,24},{24,28},{1,5},{5,9},{9,... | collective-permute-start | bytes 73736 | tf_op jit(solution)/shard_map/ppermute | solution.py:37
  38.9 69.5 %collective-permute-start.13 = (bf16[4,16,192]{1,0,2:T(4,128)(2,1)}, bf16[4,16,192]{1,0,2:T(4,128)(2,1)}, u32[]{:S(2)}, u32[]{:S(2)}) collective-permute-start(bf16[4,16,192]{1,0,2:T(4,128)(2,1)} %get-tuple-element.268), channel_id=1, source_target_pairs={{4,0},{8,4},{12,8},{16,12},{20,16},{24,20},{28,24},{5,1},{9,5},{13... | collective-permute-start | bytes 73736 | tf_op jit(solution)/shard_map/ppermute | solution.py:39
  73.0 20.3 %collective-permute-start.1 = (bf16[4,512,192]{1,2,0:T(8,128)(2,1)}, bf16[4,512,192]{1,2,0:T(8,128)(2,1)}, u32[]{:S(2)}, u32[]{:S(2)}) collective-permute-start(bf16[4,512,192]{1,2,0:T(8,128)(2,1)} %fusion.151), channel_id=1, source_target_pairs={{0,8},{4,12},{8,0},{12,4},{16,24},{20,28},{24,16},{28,20},{1,9},{5... | collective-permute-start | bytes 2359304 | tf_op jit(solution)/shard_map/ppermute | solution.py:26
  84.1 337.9 %copy-start.180 = (f32[4,64]{1,0:T(4,128)}, f32[4,64]{1,0:T(4,128)S(1)}, u32[]{:S(2)}) copy-start(f32[4,64]{1,0:T(4,128)S(1)} %maximum_convert_fusion) | copy-start | bytes 3076
  89.4 54.5 %collective-permute-start.7 = (bf16[4,1024,192]{1,0,2:T(4,128)(2,1)}, bf16[4,1024,192]{1,0,2:T(4,128)(2,1)}, u32[]{:S(2)}, u32[]{:S(2)}) collective-permute-start(bf16[4,1024,192]{1,0,2:T(4,128)(2,1)} %maximum_select_fusion.9), channel_id=1, source_target_pairs={{0,8},{4,12},{8,0},{12,4},{16,24},{20,28},{24,16},{28,20},{1,9},{5... | collective-permute-start | bytes 4718600 | tf_op jit(solution)/shard_map/ppermute | solution.py:26
  96.2 24.8 %collective-permute-start.3 = (bf16[4,512,192]{1,2,0:T(8,128)(2,1)}, bf16[4,512,192]{1,2,0:T(8,128)(2,1)}, u32[]{:S(2)}, u32[]{:S(2)}) collective-permute-start(bf16[4,512,192]{1,2,0:T(8,128)(2,1)} %get-tuple-element.277), channel_id=1, source_target_pairs={{0,4},{4,0},{8,12},{12,8},{16,20},{20,16},{24,28},{28,24},{1,5},{5... | collective-permute-start | bytes 2359304 | tf_op jit(solution)/shard_map/ppermute | solution.py:26
  111.1 371.9 %copy-start.2 = (f32[4,544,3,64]{1,3,2,0:T(8,128)}, f32[4,544,3,64]{1,3,2,0:T(8,128)S(1)}, u32[]{:S(2)}) copy-start(f32[4,544,3,64]{1,3,2,0:T(8,128)S(1)} %convert_select_fusion.1) | copy-start | bytes 5013508
  114.5 109.0 %collective-permute-start.10 = (bf16[4,1024,192]{1,0,2:T(4,128)(2,1)S(1)}, bf16[4,1024,192]{1,0,2:T(4,128)(2,1)S(1)}, u32[]{:S(2)}, u32[]{:S(2)}) collective-permute-start(bf16[4,1024,192]{1,0,2:T(4,128)(2,1)S(1)} %maximum_select_fusion.11), channel_id=1, source_target_pairs={{0,8},{4,12},{8,0},{12,4},{16,24},{20,28},{24,16},{28,20},{1,9},{5... | collective-permute-start | bytes 4718600 | tf_op jit(solution)/shard_map/ppermute | solution.py:26
  119.6 57.9 %collective-permute-start.2 = (bf16[4,512,192]{1,2,0:T(8,128)(2,1)S(1)}, bf16[4,512,192]{1,2,0:T(8,128)(2,1)S(1)}, u32[]{:S(2)}, u32[]{:S(2)}) collective-permute-start(bf16[4,512,192]{1,2,0:T(8,128)(2,1)S(1)} %copy-done.141), channel_id=1, source_target_pairs={{0,16},{4,20},{8,24},{12,28},{16,0},{20,4},{24,8},{28,12},{1,17},{... | collective-permute-start | bytes 2359304 | tf_op jit(solution)/shard_map/ppermute | solution.py:26
  122.4 97.1 %collective-permute-start.4 = (bf16[4,512,192]{1,2,0:T(8,128)(2,1)S(1)}, bf16[4,512,192]{1,2,0:T(8,128)(2,1)S(1)}, u32[]{:S(2)}, u32[]{:S(2)}) collective-permute-start(bf16[4,512,192]{1,2,0:T(8,128)(2,1)S(1)} %fusion.152), channel_id=1, source_target_pairs={{0,8},{4,12},{8,0},{12,4},{16,24},{20,28},{24,16},{28,20},{1,9},{5... | collective-permute-start | bytes 2359304 | tf_op jit(solution)/shard_map/ppermute | solution.py:26
  125.3 94.2 %copy-start.9 = (f32[4,512,192]{1,2,0:T(8,128)S(1)}, f32[4,512,192]{1,2,0:T(8,128)}, u32[]{:S(2)}) copy-start(f32[4,512,192]{1,2,0:T(8,128)} %copy-done.8) | copy-start | bytes 4718596
  125.4 94.2 %copy-start.45 = (bf16[4,512,192]{1,2,0:T(8,128)(2,1)S(1)}, bf16[4,512,192]{1,2,0:T(8,128)(2,1)}, u32[]{:S(2)}) copy-start(bf16[4,512,192]{1,2,0:T(8,128)(2,1)} %copy-done.44) | copy-start | bytes 2359300
  150.9 297.8 %collective-permute-start.8 = (bf16[4,2048,192]{1,0,2:T(4,128)(2,1)}, bf16[4,2048,192]{1,0,2:T(4,128)(2,1)}, u32[]{:S(2)}, u32[]{:S(2)}) collective-permute-start(bf16[4,2048,192]{1,0,2:T(4,128)(2,1)} %maximum_select_fusion.5), channel_id=1, source_target_pairs={{0,16},{4,20},{8,24},{12,28},{16,0},{20,4},{24,8},{28,12},{1,17},{... | collective-permute-start | bytes 9437192 | tf_op jit(solution)/shard_map/ppermute | solution.py:26
  223.5 185.1 %collective-permute-start.5 = (bf16[4,512,192]{1,2,0:T(8,128)(2,1)}, bf16[4,512,192]{1,2,0:T(8,128)(2,1)}, u32[]{:S(2)}, u32[]{:S(2)}) collective-permute-start(bf16[4,512,192]{1,2,0:T(8,128)(2,1)} %get-tuple-element.275), channel_id=1, source_target_pairs={{0,16},{4,20},{8,24},{12,28},{16,0},{20,4},{24,8},{28,12},{1,17},{... | collective-permute-start | bytes 2359304 | tf_op jit(solution)/shard_map/ppermute | solution.py:26
  227.1 243.7 %collective-permute-start.11 = (bf16[4,2048,192]{1,0,2:T(4,128)(2,1)}, bf16[4,2048,192]{1,0,2:T(4,128)(2,1)}, u32[]{:S(2)}, u32[]{:S(2)}) collective-permute-start(bf16[4,2048,192]{1,0,2:T(4,128)(2,1)} %maximum_select_fusion.7), channel_id=1, source_target_pairs={{0,16},{4,20},{8,24},{12,28},{16,0},{20,4},{24,8},{28,12},{1,17},{... | collective-permute-start | bytes 9437192 | tf_op jit(solution)/shard_map/ppermute | solution.py:26
  501.9 156.3 %all-reduce.9.cloned.1.call-start = ((), (), s32[]{:S(2)}) async-start(), calls=%async_computation.7 | async-start | bytes 6291456 | tf_op jit(solution)/shard_map/psum | solution.py:304
  589.5 163.2 %all-reduce.11.cloned.1.call-start = ((), (), s32[]{:S(2)}) async-start(), calls=%async_computation.8 | async-start | bytes 6291456 | tf_op jit(solution)/shard_map/psum | solution.py:328
  684.0 433.3 %reduce-scatter.26.cloned.1.call-start = ((), (), s32[]{:S(2)}) async-start(), calls=%async_computation.15 | async-start | bytes 884736
  779.3 43.7 %copy-start.13 = (f32[4,3,512,64]{2,3,1,0:T(8,128)}, f32[4,3,512,64]{2,3,1,0:T(8,128)S(1)}, u32[]{:S(2)}) copy-start(f32[4,3,512,64]{2,3,1,0:T(8,128)S(1)} %mul.1256) | copy-start | bytes 4718596
  780.5 19.5 %collective-permute-start.14 = (bf16[4,3,512,64]{2,3,1,0:T(8,128)(2,1)}, bf16[4,3,512,64]{2,3,1,0:T(8,128)(2,1)}, u32[]{:S(2)}, u32[]{:S(2)}) collective-permute-start(bf16[4,3,512,64]{2,3,1,0:T(8,128)(2,1)} %multiply_convert_fusion.5), channel_id=1, source_target_pairs={{0,4},{4,0},{8,12},{12,8},{16,20},{20,16},{24,28},{28,24},{1,5},{5... | collective-permute-start | bytes 2359304 | tf_op jit(solution)/shard_map/ppermute | solution.py:26
  802.3 20.7 %collective-permute-start.15 = (bf16[4,3,512,64]{2,3,1,0:T(8,128)(2,1)}, bf16[4,3,512,64]{2,3,1,0:T(8,128)(2,1)}, u32[]{:S(2)}, u32[]{:S(2)}) collective-permute-start(bf16[4,3,512,64]{2,3,1,0:T(8,128)(2,1)} %fusion.153), channel_id=1, source_target_pairs={{0,8},{4,12},{8,0},{12,4},{16,24},{20,28},{24,16},{28,20},{1,9},{5... | collective-permute-start | bytes 2359304 | tf_op jit(solution)/shard_map/ppermute | solution.py:26
  804.7 30.0 %collective-permute-start.26 = (bf16[4,16,192]{1,2,0:T(8,128)(2,1)}, bf16[4,16,192]{1,2,0:T(8,128)(2,1)S(1)}, u32[]{:S(2)}, u32[]{:S(2)}) collective-permute-start(bf16[4,16,192]{1,2,0:T(8,128)(2,1)} %copy.1011), channel_id=1, source_target_pairs={{0,4},{4,8},{8,12},{12,16},{16,20},{20,24},{24,28},{1,5},{5,9},{9,... | collective-permute-start | bytes 73736 | tf_op jit(solution)/shard_map/ppermute | solution.py:37
  808.8 26.0 %collective-permute-start.27 = (bf16[4,16,192]{1,2,0:T(8,128)(2,1)}, bf16[4,16,192]{1,2,0:T(8,128)(2,1)S(1)}, u32[]{:S(2)}, u32[]{:S(2)}) collective-permute-start(bf16[4,16,192]{1,2,0:T(8,128)(2,1)} %copy.1012), channel_id=1, source_target_pairs={{4,0},{8,4},{12,8},{16,12},{20,16},{24,20},{28,24},{5,1},{9,5},{13... | collective-permute-start | bytes 73736 | tf_op jit(solution)/shard_map/ppermute | solution.py:39
  825.6 39.4 %collective-permute-start.16 = (bf16[4,3,512,64]{2,3,1,0:T(8,128)(2,1)}, bf16[4,3,512,64]{2,3,1,0:T(8,128)(2,1)}, u32[]{:S(2)}, u32[]{:S(2)}) collective-permute-start(bf16[4,3,512,64]{2,3,1,0:T(8,128)(2,1)} %fusion.121), channel_id=1, source_target_pairs={{0,16},{4,20},{8,24},{12,28},{16,0},{20,4},{24,8},{28,12},{1,17},{... | collective-permute-start | bytes 2359304 | tf_op jit(solution)/shard_map/ppermute | solution.py:26
  834.7 324.6 %all-reduce.13.cloned.1.call-start = ((), (), s32[]{:S(2)}) async-start(), calls=%async_computation.9 | async-start | bytes 6291456 | tf_op jit(solution)/shard_map/psum | solution.py:479
  915.2 3.9 collective-permute-start.17
  919.1 3.9 collective-permute-start.18
  923.0 4.8 collective-permute-start.19
  938.4 16.8 %collective-permute-start.20 = (bf16[4,512,192]{1,2,0:T(8,128)(2,1)S(1)}, bf16[4,512,192]{1,2,0:T(8,128)(2,1)S(1)}, u32[]{:S(2)}, u32[]{:S(2)}) collective-permute-start(bf16[4,512,192]{1,2,0:T(8,128)(2,1)S(1)} %multiply_convert_fusion.4), channel_id=1, source_target_pairs={{0,4},{4,0},{8,12},{12,8},{16,20},{20,16},{24,28},{28,24},{1,5},{5... | collective-permute-start | bytes 2359304 | tf_op jit(solution)/shard_map/ppermute | solution.py:26
  955.5 15.9 %collective-permute-start.21 = (bf16[4,512,192]{1,2,0:T(8,128)(2,1)S(1)}, bf16[4,512,192]{1,2,0:T(8,128)(2,1)S(1)}, u32[]{:S(2)}, u32[]{:S(2)}) collective-permute-start(bf16[4,512,192]{1,2,0:T(8,128)(2,1)S(1)} %fusion.154), channel_id=1, source_target_pairs={{0,8},{4,12},{8,0},{12,4},{16,24},{20,28},{24,16},{28,20},{1,9},{5... | collective-permute-start | bytes 2359304 | tf_op jit(solution)/shard_map/ppermute | solution.py:26
  972.0 15.0 %collective-permute-start.23 = (bf16[4,512,192]{1,2,0:T(8,128)(2,1)S(1)}, bf16[4,512,192]{1,2,0:T(8,128)(2,1)S(1)}, u32[]{:S(2)}, u32[]{:S(2)}) collective-permute-start(bf16[4,512,192]{1,2,0:T(8,128)(2,1)S(1)} %get-tuple-element.273), channel_id=1, source_target_pairs={{0,4},{4,0},{8,12},{12,8},{16,20},{20,16},{24,28},{28,24},{1,5},{5... | collective-permute-start | bytes 2359304 | tf_op jit(solution)/shard_map/ppermute | solution.py:26
  973.8 49.1 %copy-start.80 = (f32[4,3,64,64]{2,3,1,0:T(8,128)}, f32[4,3,64,64]{2,3,1,0:T(8,128)S(1)}, u32[]{:S(2)}) copy-start(f32[4,3,64,64]{2,3,1,0:T(8,128)S(1)} %get-tuple-element.256) | copy-start | bytes 589828
  973.8 49.0 %copy-start.165 = (f32[4,3,64]{2,1,0:T(4,128)}, f32[4,3,64]{2,1,0:T(4,128)S(1)}, u32[]{:S(2)}) copy-start(f32[4,3,64]{2,1,0:T(4,128)S(1)} %negate_divide_fusion) | copy-start | bytes 9220
  974.2 33.2 %collective-permute-start.22 = (bf16[4,512,192]{1,2,0:T(8,128)(2,1)S(1)}, bf16[4,512,192]{1,2,0:T(8,128)(2,1)}, u32[]{:S(2)}, u32[]{:S(2)}) collective-permute-start(bf16[4,512,192]{1,2,0:T(8,128)(2,1)S(1)} %get-tuple-element.272), channel_id=1, source_target_pairs={{0,16},{4,20},{8,24},{12,28},{16,0},{20,4},{24,8},{28,12},{1,17},{... | collective-permute-start | bytes 2359304 | tf_op jit(solution)/shard_map/ppermute | solution.py:26
  987.3 30.8 %collective-permute-start.24 = (bf16[4,512,192]{1,2,0:T(8,128)(2,1)S(1)}, bf16[4,512,192]{1,2,0:T(8,128)(2,1)S(1)}, u32[]{:S(2)}, u32[]{:S(2)}) collective-permute-start(bf16[4,512,192]{1,2,0:T(8,128)(2,1)S(1)} %fusion.155), channel_id=1, source_target_pairs={{0,8},{4,12},{8,0},{12,4},{16,24},{20,28},{24,16},{28,20},{1,9},{5... | collective-permute-start | bytes 2359304 | tf_op jit(solution)/shard_map/ppermute | solution.py:26
  1022.0 33.3 %collective-permute-start.25 = (bf16[4,512,192]{1,2,0:T(8,128)(2,1)}, bf16[4,512,192]{1,2,0:T(8,128)(2,1)}, u32[]{:S(2)}, u32[]{:S(2)}) collective-permute-start(bf16[4,512,192]{1,2,0:T(8,128)(2,1)} %get-tuple-element.271), channel_id=1, source_target_pairs={{0,16},{4,20},{8,24},{12,28},{16,0},{20,4},{24,8},{28,12},{1,17},{... | collective-permute-start | bytes 2359304 | tf_op jit(solution)/shard_map/ppermute | solution.py:26
  1072.7 141.1 %reduce-scatter.18.cloned.1.call-start = ((), (), s32[]{:S(2)}) async-start(), calls=%async_computation.11 | async-start | bytes 2654208 | tf_op jit(solution)/shard_map/reduce_scatter | solution.py:494
  1080.7 205.7 %reduce-scatter.16.cloned.1.call-start = ((), (), s32[]{:S(2)}) async-start(), calls=%async_computation.10 | async-start | bytes 2654208 | tf_op jit(solution)/shard_map/reduce_scatter | solution.py:493
  1088.7 263.6 %reduce-scatter.24.cloned.1.call-start = ((), (), s32[]{:S(2)}) async-start(), calls=%async_computation.14 | async-start | bytes 884736
  1092.7 325.1 %reduce-scatter.22.cloned.1.call-start = ((), (), s32[]{:S(2)}) async-start(), calls=%async_computation.13 | async-start | bytes 884736
  1099.9 383.3 %reduce-scatter.20.cloned.1.call-start = ((), (), s32[]{:S(2)}) async-start(), calls=%async_computation.12 | async-start | bytes 884736
  1159.3 324.0 %copy-start.1 = (bf16[768,768]{1,0:T(8,128)(2,1)S(1)}, bf16[768,768]{1,0:T(8,128)(2,1)}, u32[]{:S(2)}) copy-start(bf16[768,768]{1,0:T(8,128)(2,1)} %param.30) | copy-start | bytes 3538948
  (277 other events, 1820.0 us)
Sparse Core Ops, SparseCore 0:
  502.0 68.5 all-reduce.6
  589.6 68.5 all-reduce.8
  684.1 68.5 all-reduce.10
  834.8 64.0 reduce-scatter.25
  1072.8 67.4 all-reduce.12
  1144.6 69.1 reduce-scatter.17
  1218.3 68.1 reduce-scatter.15
  1290.7 61.6 reduce-scatter.23
  1356.2 61.4 reduce-scatter.21
  1421.8 61.3 reduce-scatter.19
where the time goes:
time: 1500 us; the launch traced here: 1490 us
  waiting for transfers between devices  916 us (61%)
  matrix products  188 us (13%)
  other arithmetic  158 us (11%)
  local copies, waits for them, and re-layouts  125 us (8%)
  starting transfers between devices  48.6 us (3%)
  blocking collectives  35.1 us (2%)
  between operations  19.4 us (1%)
    ppermute x24, waiting for transfers between devices, swapped(): lax.ppermute(shard, axis, [(i, i ^ 1 << distance) for i in range(lax.axis...  398 us
    unnamed x14, waiting for transfers between devices  197 us
    reduce_scatter x1, waiting for transfers between devices, per_device(): lax.psum_scatter(grad_up_weight, 'seq', scatter_dimension=0, tiled=True)  72.6 us
    psum x1, waiting for transfers between devices, per_device(): lax.psum(jnp.einsum('tf,df->td', back_hidden, up_weight, preferred_elemen...  68.6 us
    psum x1, waiting for transfers between devices, per_device(): lax.psum(jnp.dot(context, output_weight, preferred_element_type=jnp.float...  68.1 us
    psum x1, waiting for transfers between devices, per_device(): lax.psum(jnp.dot(active_low, down_weight, preferred_element_type=jnp.floa...  64 us
    reduce_scatter x1, waiting for transfers between devices, per_device(): lax.psum_scatter(grad_down_weight, 'seq', scatter_dimension=1, tiled=True)  47.4 us
    ppermute x24, starting transfers between devices, swapped(): lax.ppermute(shard, axis, [(i, i ^ 1 << distance) for i in range(lax.axis...  39.2 us
  transfers between devices with their start and end apart: 38, of which 27 were waited for; matrix products, arithmetic and copies ran while one was open for 23% of the time, Pallas kernels for 0%

commit v1 on v0

v1 whole, which is shorter than its diff:
```python
import jax
import jax.numpy as jnp
from jax import lax
from jax.sharding import PartitionSpec as P

HEAD_DIM = 64
TAPS = 33
SWEEPS = 6
SPAN = 4096
LANES = 128


highest = lax.Precision.HIGHEST
epsilon = 1e-05
very_negative = -1e30
f32 = jnp.float32
bf16 = jnp.bfloat16


def swap(value, axis, step):
    return lax.ppermute(value, axis, [(i, i ^ step) for i in range(lax.axis_size(axis))])


def dot(a, b):
    return jnp.dot(a, b, preferred_element_type=f32)


def outer(a, b):
    return lax.dot_general(a, b, (((0,), (0,)), ((), ())), preferred_element_type=f32)


def dot_t(a, b):
    return lax.dot_general(a, b, (((1,), (1,)), ((), ())), preferred_element_type=f32)


def rounded(value):
    return lax.reduce_precision(value, 8, 7)


def count_below(ends, positions):
    return jnp.sum((ends[None, :] <= positions[:, None]).astype(jnp.int32), axis=1)


def spread_shards(shard):
    core = swap(shard, "tp", 1)
    far = swap(shard, "tp", 2)
    return (shard, core, far, swap(far, "tp", 1))


def segment_exchange(state, index, item_of, levels, pack, unpack, merge):
    own_item = item_of[index]
    own = left_edge = right_edge = state
    for level in range(levels):
        size = 1 << level
        start = (index >> level) << level
        other = start ^ size
        is_left = (index & size) == 0

        def choose(a, b):
            return jax.tree.map(lambda x, y: jnp.where(is_left, x, y), a, b)

        far_edge_item = jnp.where(is_left, item_of[other], item_of[other + size - 1])
        far_outer_item = jnp.where(is_left, item_of[other + size - 1], item_of[other])
        facing_item = jnp.where(is_left, item_of[start + size - 1], item_of[start])
        outer_item = jnp.where(is_left, item_of[start], item_of[start + size - 1])
        last = level == levels - 1
        if level == 0:
            facing = outer_edge = state
            got = unpack(swap(pack(state), "seq", size))
            far_facing = far_outer = got
        else:
            facing = choose(right_edge, left_edge)
            outer_edge = choose(left_edge, right_edge)
            if last:
                far_facing = far_outer = unpack(swap(pack(facing), "seq", size))
            else:
                got = swap((pack(facing), pack(outer_edge)), "seq", size)
                far_facing, far_outer = unpack(got[0]), unpack(got[1])
        own = merge(own, far_facing, own_item == far_edge_item)
        if not last:
            near = merge(outer_edge, far_facing, outer_item == far_edge_item)
            away = merge(far_outer, facing, far_outer_item == facing_item)
            left_edge = choose(near, away)
            right_edge = choose(away, near)
    return own


def add_where(a, b, use):
    return a + jnp.where(use, b, 0.0)


def segment_sum(value, index, item_of, levels):
    return segment_exchange(
        value,
        index,
        item_of,
        levels,
        lambda v: v.astype(bf16),
        lambda v: v.astype(f32),
        add_where,
    )


def soft_pack(state):
    mixed, top, total = state
    high = rounded(total)
    low = total - high
    heads = top.shape[1]
    pad = jnp.zeros((top.shape[0], LANES - 3 * heads), f32)
    return jnp.concatenate((mixed, top, high, low, pad), axis=1).astype(bf16)


def soft_unpack(heads, width):
    def unpack(message):
        message = message.astype(f32)
        return (
            message[:, :width],
            message[:, width : width + heads],
            message[:, width + heads : width + 2 * heads]
            + message[:, width + 2 * heads : width + 3 * heads],
        )

    return unpack


def soft_merge(a, b, use):
    mixed_a, top_a, total_a = a
    mixed_b, top_b, total_b = b
    top = jnp.where(use, jnp.maximum(top_a, top_b), top_a)
    scale_a = jnp.exp(top_a - top)
    scale_b = jnp.where(use, jnp.exp(jnp.where(use, top_b - top, 0.0)), 0.0)
    wide_a = jnp.repeat(scale_a, HEAD_DIM, axis=1)
    wide_b = jnp.repeat(scale_b, HEAD_DIM, axis=1)
    return (mixed_a * wide_a + mixed_b * wide_b, top, total_a * scale_a + total_b * scale_b)


def scatter_weight(blocks, seq_index):
    blocks = [b.astype(bf16) for b in blocks]
    got = swap((blocks[1], blocks[3]), "tp", 1)
    mine = blocks[0].astype(f32) + got[0].astype(f32)
    away = (blocks[2].astype(f32) + got[1].astype(f32)).astype(bf16)
    total = mine + swap(away, "tp", 2).astype(f32)
    count = lax.axis_size("seq")
    rows, columns = total.shape
    size = 1
    total = total.reshape(count, rows // count, columns)
    while size < count:
        bit = (seq_index // size) % 2
        view = total.reshape(total.shape[0] // 2, 2, rows // count, columns)
        keep = lax.dynamic_index_in_dim(view, bit, axis=1, keepdims=False)
        send = lax.dynamic_index_in_dim(view, 1 - bit, axis=1, keepdims=False).astype(bf16)
        total = keep + swap(send, "seq", size).astype(f32)
        size *= 2
    return total[0]


def sum_everywhere(value):
    for axis in ("tp", "seq"):
        size = 1
        while size < lax.axis_size(axis):
            value = value + swap(value, axis, size)
            size *= 2
    return value


def newton_inverse(kernel):
    size = kernel.shape[-1]
    column_sums = jnp.sum(kernel, axis=-2)
    bound = jnp.sqrt(jnp.sum(column_sums * column_sums, axis=-1))[..., None, None]
    identity = jnp.eye(size, dtype=kernel.dtype)
    inverse = jnp.swapaxes(kernel, -1, -2) / bound
    for sweep in range(SWEEPS):
        product = jnp.matmul(kernel, inverse, precision=highest)
        inner = 7.0 * identity - product
        inner = 15.0 * identity - jnp.matmul(product, inner, precision=highest)
        inner = 13.0 * identity - jnp.matmul(product, inner, precision=highest)
        inverse = 0.25 * jnp.matmul(inverse, inner, precision=highest)
    return inverse


def landmark_core(land_query, land_key, mixed_values):
    scores = jnp.einsum("mhd,nhd->hmn", land_query, land_key, precision=highest)
    powers = jnp.exp(scores - jnp.max(scores, axis=-1, keepdims=True))
    kernel = powers / jnp.sum(powers, axis=-1, keepdims=True)
    return jnp.einsum("hmn,hnd->hmd", newton_inverse(kernel), mixed_values, precision=highest)


def layer_norm(values, gain, shift):
    centred = values - jnp.mean(values, axis=-1, keepdims=True)
    inverse = lax.rsqrt(jnp.mean(centred * centred, axis=-1, keepdims=True) + epsilon)
    normed = centred * inverse
    return (normed * gain + shift, normed, inverse)


def norm_back(upstream, gain, normed, inverse):
    scaled = upstream * gain
    centred = scaled - jnp.mean(scaled, axis=-1, keepdims=True)
    return (centred - normed * jnp.mean(scaled * normed, axis=-1, keepdims=True)) * inverse


def gelu(values):
    return 0.5 * values * (1.0 + lax.erf(values * 0.7071067811865476))


def per_device(
    tokens,
    query_weight,
    query_bias,
    key_weight,
    value_weight,
    value_bias,
    conv_weight,
    output_weight,
    output_bias,
    first_gain,
    first_shift,
    up_weight,
    up_bias,
    down_weight,
    down_bias,
    second_gain,
    second_shift,
    segment_sizes,
    cotangent,
):
    rows, width, model = tokens.shape
    channels = query_weight.shape[1]
    ranks = lax.axis_size("tp")
    own_heads = channels // HEAD_DIM
    heads = ranks * own_heads
    hidden_units = up_weight.shape[1]
    items = segment_sizes.shape[1]
    marks = segment_sizes.shape[2]
    reach = TAPS // 2
    scale = HEAD_DIM ** (-0.25)
    group = SPAN // width
    levels = group.bit_length() - 1
    device = lax.axis_index("seq")
    rank = lax.axis_index("tp")
    local_index = device % group
    group_number = device // group
    groups = segment_sizes.shape[0] // rows
    start = local_index * width

    row_sizes = lax.dynamic_index_in_dim(
        segment_sizes, rank * groups + group_number, axis=0, keepdims=False
    )
    item_ends = jnp.cumsum(jnp.sum(row_sizes, axis=1))
    item_of = count_below(item_ends, width * jnp.arange(group, dtype=jnp.int32))
    own_item = item_of[local_index]
    slot_ends = jnp.cumsum(row_sizes.reshape(-1))
    positions = start + jnp.arange(width, dtype=jnp.int32)
    token_mark = count_below(slot_ends, positions) - own_item * marks
    own_sizes = lax.dynamic_index_in_dim(row_sizes, own_item, axis=0, keepdims=False)
    own_count = jnp.maximum(own_sizes, 1).astype(f32)[:, None]
    member = token_mark[:, None] == jnp.arange(marks, dtype=jnp.int32)[None, :]
    member_low = member.astype(bf16)

    def by_rank(stacked):
        return jnp.take(stacked, jnp.arange(ranks) ^ rank, axis=0)

    small = jnp.concatenate(
        (
            query_bias.reshape(-1),
            value_bias.reshape(-1),
            conv_weight.reshape(-1),
            up_bias.reshape(-1),
        )
    )
    wide = 2 * channels
    small_rows = -(-small.shape[0] // wide)
    small_rows += -small_rows % 16
    small = jnp.pad(small, (0, small_rows * wide - small.shape[0])).reshape(small_rows, wide)
    query_key = jnp.concatenate(
        (jnp.concatenate((query_weight, key_weight), axis=1), small), axis=0
    )
    query_key = spread_shards(query_key)
    value_blocks = spread_shards(value_weight)
    output_blocks = spread_shards(output_weight)
    up_blocks = spread_shards(up_weight)
    down_blocks = spread_shards(down_weight)
    smalls = [block[model:].reshape(-1).astype(f32) for block in query_key]
    query_bias_all = jnp.concatenate([s[:channels] for s in smalls])
    value_bias_all = jnp.concatenate([s[channels : 2 * channels] for s in smalls])
    taps_all = jnp.concatenate(
        [s[2 * channels : 2 * channels + own_heads * TAPS].reshape(own_heads, TAPS) for s in smalls]
    )
    up_start = 2 * channels + own_heads * TAPS
    up_bias_all = [s[up_start : up_start + hidden_units] for s in smalls]

    flat = lax.dynamic_index_in_dim(tokens, rank, axis=0, keepdims=False)
    upstream = lax.dynamic_index_in_dim(cotangent, rank, axis=0, keepdims=False).astype(f32)
    products = [dot(flat, block[:model]) for block in query_key]
    query = (
        scale * (jnp.concatenate([p[:, :channels] for p in products], axis=1) + query_bias_all)
    ).astype(bf16)
    keys = (scale * jnp.concatenate([p[:, channels:] for p in products], axis=1)).astype(bf16)
    part = outer(member_low, jnp.concatenate((query, keys), axis=1))
    sums = segment_sum(part, local_index, item_of, levels)
    land = (sums / own_count).astype(bf16)
    land_query, land_key = land[:, :model], land[:, model:]
    values = (
        jnp.concatenate([dot(flat, block) for block in value_blocks], axis=1) + value_bias_all
    ).astype(bf16)

    def split_heads(array):
        return array.reshape(array.shape[0], heads, HEAD_DIM)

    def neighbours(cells):
        count = lax.axis_size("seq")
        before = lax.ppermute(cells[width - reach :], "seq", [(i, i + 1) for i in range(count - 1)])
        after = lax.ppermute(cells[:reach], "seq", [(i + 1, i) for i in range(count - 1)])
        return jnp.concatenate((before, cells, after), axis=0)

    value_rim = neighbours(values)
    query_heads = split_heads(query)
    key_heads = split_heads(keys)
    value_heads = split_heads(values)
    land_query_heads = split_heads(land_query)
    land_key_heads = split_heads(land_key)

    key_scores = jnp.einsum(
        "mhd,thd->hmt", land_query_heads, key_heads, preferred_element_type=f32
    )
    local_top = rounded(jnp.max(key_scores, axis=-1))
    powers = jnp.exp(key_scores - local_top[..., None])
    part_mixed = jnp.einsum(
        "hmt,thd->mhd", powers.astype(bf16), value_heads, preferred_element_type=f32
    ).reshape(marks, model)
    mixed, key_top, key_total = segment_exchange(
        (part_mixed, local_top.T, jnp.sum(powers, axis=-1).T),
        local_index,
        item_of,
        levels,
        soft_pack,
        soft_unpack(heads, model),
        soft_merge,
    )
    mixed_values = mixed.reshape(marks, heads, HEAD_DIM) / key_total[:, :, None]
    mixed_values = mixed_values.transpose(1, 0, 2)

    token_scores = jnp.einsum(
        "thd,mhd->htm", query_heads, land_key_heads, preferred_element_type=f32
    )
    token_powers = jnp.exp(token_scores - jnp.max(token_scores, axis=-1, keepdims=True))
    token_weights = token_powers / jnp.sum(token_powers, axis=-1, keepdims=True)
    token_low = token_weights.astype(bf16)

    mixed_land, core_back = jax.vjp(
        landmark_core, land_query_heads.astype(f32), land_key_heads.astype(f32), mixed_values
    )
    mixed_low = mixed_land.astype(bf16)
    nystrom = jnp.einsum("htm,hmd->thd", token_low, mixed_low, preferred_element_type=f32)

    rim_pos = start - reach + jnp.arange(width + 2 * reach, dtype=jnp.int32)
    rim_item = count_below(item_ends, jnp.clip(rim_pos, 0, SPAN - 1))
    rim_keep = ((rim_pos >= 0) & (rim_pos < SPAN) & (rim_item == own_item))[:, None]
    kept_values = jnp.where(rim_keep, value_rim, 0).astype(f32)
    taps_wide = jnp.repeat(taps_all, HEAD_DIM, axis=0).T
    convolved = jnp.zeros((width, model), f32)
    for offset in range(TAPS):
        convolved = convolved + kept_values[offset : offset + width] * taps_wide[offset][None, :]
    context = (nystrom.reshape(width, model) + convolved).astype(bf16)
    output_all = jnp.concatenate(output_blocks, axis=0)
    attention = dot(context, output_all) + output_bias.astype(f32)
    first_gain32 = first_gain.astype(f32)
    second_gain32 = second_gain.astype(f32)
    first_out, first_normed, first_inverse = layer_norm(
        flat.astype(f32) + attention, first_gain32, first_shift.astype(f32)
    )
    first_low = first_out.astype(bf16)
    hidden = [dot(first_low, w) + b for w, b in zip(up_blocks, up_bias_all)]
    active = [gelu(h).astype(bf16) for h in hidden]
    feed = down_bias.astype(f32)
    for a, w in zip(active, down_blocks):
        feed = feed + dot(a, w)
    layer_out, second_normed, second_inverse = layer_norm(
        first_out + feed, second_gain32, second_shift.astype(f32)
    )
    grad_second_gain = jnp.sum(upstream * second_normed, axis=0)
    grad_second_shift = jnp.sum(upstream, axis=0)
    back_second = norm_back(upstream, second_gain32, second_normed, second_inverse)
    back_feed = back_second.astype(bf16)
    grad_down_bias = jnp.sum(back_feed.astype(f32), axis=0)
    grad_down_weight = scatter_weight([outer(back_feed, a) for a in active], device)
    back_hidden = [
        jax.vjp(gelu, h)[1](dot_t(back_feed, w))[0].astype(bf16)
        for h, w in zip(hidden, down_blocks)
    ]
    grad_up_bias = [jnp.sum(b.astype(f32), axis=0) for b in back_hidden]
    grad_up_weight = scatter_weight([outer(first_low, b) for b in back_hidden], device)
    back_first = back_second
    for b, w in zip(back_hidden, up_blocks):
        back_first = back_first + dot_t(b, w)
    grad_first_gain = jnp.sum(back_first * first_normed, axis=0)
    grad_first_shift = jnp.sum(back_first, axis=0)
    back_input = norm_back(back_first, first_gain32, first_normed, first_inverse)
    back_attention = back_input.astype(bf16)
    grad_output_bias = jnp.sum(back_attention.astype(f32), axis=0)
    context_parts = [context[:, r * channels : (r + 1) * channels] for r in range(ranks)]
    grad_output_weight = scatter_weight([outer(back_attention, c) for c in context_parts], device)
    back_context = dot_t(back_attention, output_all).astype(bf16)

    context_rim = neighbours(back_context)
    kept_back = jnp.where(rim_keep, context_rim, 0).astype(f32)
    back_wide = back_context.astype(f32)
    conv_values = jnp.zeros((width, model), f32)
    tap_terms = []
    for offset in range(TAPS):
        lower = 2 * reach - offset
        conv_values = conv_values + kept_back[lower : lower + width] * taps_wide[offset][None, :]
        tap_terms.append(jnp.sum(back_wide * kept_values[offset : offset + width], axis=0))
    conv_part = jnp.sum(jnp.stack(tap_terms, axis=1).reshape(heads, HEAD_DIM, TAPS), axis=1)

    back_heads = split_heads(back_context)
    part_back = jnp.einsum(
        "htm,thd->mhd", token_low, back_heads, preferred_element_type=f32
    ).reshape(marks, model)
    back_token = jnp.einsum("thd,hmd->htm", back_heads, mixed_low, preferred_element_type=f32)
    back_token_scores = (
        token_weights * (back_token - jnp.sum(token_weights * back_token, axis=-1, keepdims=True))
    ).astype(bf16)
    back_query_token = jnp.einsum(
        "htm,mhd->thd", back_token_scores, land_key_heads, preferred_element_type=f32
    ).reshape(width, model)
    part_land_key = jnp.einsum(
        "htm,thd->mhd", back_token_scores, query_heads, preferred_element_type=f32
    ).reshape(marks, model)
    back_mixed_land = segment_sum(part_back, local_index, item_of, levels)
    sum_land_key = segment_sum(part_land_key, local_index, item_of, levels)
    back_land_query_a, back_land_key_a, back_mixed = core_back(
        back_mixed_land.reshape(marks, heads, HEAD_DIM).transpose(1, 0, 2)
    )
    back_mixed_low = back_mixed.astype(bf16)
    key_weights = jnp.exp(key_scores - key_top.T[..., None]) / key_total.T[..., None]
    back_key_weights = jnp.einsum(
        "hmd,thd->hmt", back_mixed_low, value_heads, preferred_element_type=f32
    )
    key_dots = jnp.sum(back_mixed_low.astype(f32) * mixed_values, axis=-1)
    back_key_scores = (key_weights * (back_key_weights - key_dots[..., None])).astype(bf16)
    part_land_query = jnp.einsum(
        "hmt,thd->mhd", back_key_scores, key_heads, preferred_element_type=f32
    ).reshape(marks, model)
    sum_land_query = segment_sum(part_land_query, local_index, item_of, levels)
    back_key_direct = jnp.einsum(
        "hmt,mhd->thd", back_key_scores, land_query_heads, preferred_element_type=f32
    ).reshape(width, model)
    back_value_direct = jnp.einsum(
        "hmt,hmd->thd", key_weights.astype(bf16), back_mixed_low, preferred_element_type=f32
    ).reshape(width, model)
    back_values = (back_value_direct + conv_values).astype(bf16)
    back_land_query = sum_land_query + back_land_query_a.reshape(marks, model)
    back_land_key = sum_land_key + back_land_key_a.reshape(marks, model)
    member_wide = member.astype(f32)
    back_query = (
        back_query_token + jnp.dot(member_wide, back_land_query / own_count, precision=highest)
    ).astype(bf16)
    back_keys = (
        back_key_direct + jnp.dot(member_wide, back_land_key / own_count, precision=highest)
    ).astype(bf16)

    def block(array, r):
        return array[:, r * channels : (r + 1) * channels]

    projection = [
        jnp.concatenate(
            (
                scale * outer(flat, block(back_query, r)),
                scale * outer(flat, block(back_keys, r)),
                outer(flat, block(back_values, r)),
            ),
            axis=1,
        )
        for r in range(ranks)
    ]
    grad_projection = scatter_weight(projection, device)
    projected = jnp.zeros((width, model), f32)
    for r in range(ranks):
        both = jnp.concatenate((block(back_query, r), block(back_keys, r)), axis=1)
        projected = projected + scale * dot_t(both, query_key[r][:model])
        projected = projected + dot_t(block(back_values, r), value_blocks[r])
    grad_rows = jnp.stack(spread_shards((back_input + projected).astype(bf16)))
    grad_tokens = by_rank(grad_rows).astype(f32)
    layer_rows = by_rank(jnp.stack(spread_shards(layer_out.astype(bf16))))

    ranked = jnp.stack(
        [
            jnp.concatenate(
                (
                    grad_up_bias[r],
                    jnp.sum(block(back_values, r).astype(f32), axis=0),
                    scale * jnp.sum(block(back_query, r).astype(f32), axis=0),
                    conv_part[r * own_heads : (r + 1) * own_heads].reshape(-1),
                )
            )
            for r in range(ranks)
        ]
    )
    ranked = by_rank(ranked)
    ranked_size = ranked.size
    shared = [
        grad_output_bias,
        grad_first_gain,
        grad_first_shift,
        grad_down_bias,
        grad_second_gain,
        grad_second_shift,
    ]
    bundle = jnp.concatenate([ranked.reshape(-1)] + shared)
    bundle = jnp.pad(bundle, (0, -bundle.shape[0] % (8 * LANES))).reshape(-1, LANES)
    bundle = sum_everywhere(bundle).reshape(-1)
    own_ranked = lax.dynamic_index_in_dim(
        bundle[:ranked_size].reshape(ranks, -1), rank, axis=0, keepdims=False
    )
    grad_up_bias = own_ranked[:hidden_units]
    at = hidden_units
    grad_value_bias = own_ranked[at : at + channels].reshape(own_heads, HEAD_DIM)
    at += channels
    share = HEAD_DIM // lax.axis_size("seq")
    grad_query_bias = lax.dynamic_slice_in_dim(
        own_ranked[at : at + channels].reshape(own_heads, HEAD_DIM), device * share, share, axis=1
    )
    at += channels
    grad_conv_weight = own_ranked[at : at + own_heads * TAPS].reshape(own_heads, TAPS)
    shared = [
        bundle[ranked_size + k * model : ranked_size + (k + 1) * model] for k in range(len(shared))
    ]
    return (
        layer_rows,
        grad_tokens,
        grad_projection[:, :channels],
        grad_query_bias,
        grad_projection[:, channels : 2 * channels],
        grad_projection[:, 2 * channels :],
        grad_value_bias,
        grad_conv_weight,
        grad_output_weight.T,
        shared[0],
        shared[1],
        shared[2],
        grad_up_weight,
        grad_up_bias,
        grad_down_weight.T,
        shared[3],
        shared[4],
        shared[5],
    )


def solution(mesh):
    placed = (
        P(None, "seq", None),
        P(None, "tp"),
        P("tp", None),
        P(None, "tp"),
        P(None, "tp"),
        P("tp", None),
        P("tp", None),
        P("tp", None),
        P(),
        P(),
        P(),
        P(None, "tp"),
        P("tp"),
        P("tp", None),
        P(),
        P(),
        P(),
        P(),
        P(None, "seq", None),
    )
    return jax.shard_map(
        per_device,
        mesh=mesh,
        in_specs=placed,
        out_specs=(
            P(None, "seq", None),
            P(None, "seq", None),
            P("seq", "tp"),
            P("tp", "seq"),
            P("seq", "tp"),
            P("seq", "tp"),
            P("tp", None),
            P("tp", None),
            P("tp", "seq"),
            P(),
            P(),
            P(),
            P("seq", "tp"),
            P("tp"),
            P("tp", "seq"),
            P(),
            P(),
            P(),
        ),
        check_vma=False,
    )
```

time: 1500 us -> 727 us (0.48)
  waiting for transfers between devices: 916 us -> 120 us
  blocking collectives: 35.1 us -> 0 us
  local copies, waits for them, and re-layouts: 125 us -> 157 us
  starting transfers between devices: 48.6 us -> 73.4 us
  other arithmetic: 158 us -> 142 us
    ppermute x28 -> x74, waiting for transfers between devices: 398 us -> 120 us  [the longest x70 119 us: swap(): lax.ppermute(value, axis, [(i, i ^ step) for i in range(lax.axis_size(axi...]
    psum x4 -> x0, waiting for transfers between devices: 201 us -> none  [the longest x1 68.6 us: per_device(): lax.psum(jnp.einsum('tf,df->td', back_hidden, up_weight, preferred_elemen...]
    unnamed x14 -> x0, waiting for transfers between devices: 197 us -> none
    reduce_scatter x2 -> x0, waiting for transfers between devices: 120 us -> none  [the longest x1 72.6 us: per_device(): lax.psum_scatter(grad_up_weight, 'seq', scatter_dimension=0, tiled=True)]
    convert_element_type x23 -> x37, other arithmetic: 20.2 us -> 67.1 us  [the longest x1 20.3 us: per_device(): back_values = (back_value_direct + conv_values).astype(bf16)]
    unnamed x1 -> x0, blocking collectives: 35.1 us -> none
    reduce_sum x16 -> x11, other arithmetic: 54.7 us -> 19.8 us  [the longest x1 11.2 us: per_device(): jnp.sum(back_wide * kept_values[offset:offset + width], axis=0)]
    select_n x11 -> x3, other arithmetic: 29.3 us -> 1.42 us  [by_rank(): return jnp.take(stacked, jnp.arange(ranks) ^ rank, axis=0)]
  transfers between devices with their start and end apart: 38 -> 74, of which waited for: 27 -> 26; matrix products, arithmetic and copies ran while one was open for 23% -> 57% of each run, Pallas kernels for 0% -> 0%
where the time goes in v1:
time: 727 us; the launch traced here: 714 us
  matrix products  201 us (28%)
  local copies, waits for them, and re-layouts  157 us (22%)
  other arithmetic  142 us (20%)
  waiting for transfers between devices  120 us (17%)
  starting transfers between devices  73.4 us (10%)
  between operations  20.5 us (3%)
    ppermute x70, waiting for transfers between devices, swap(): lax.ppermute(value, axis, [(i, i ^ step) for i in range(lax.axis_size(axi...  119 us
    ppermute x70, starting transfers between devices, swap(): lax.ppermute(value, axis, [(i, i ^ step) for i in range(lax.axis_size(axi...  62.6 us
    dot_general x17, matrix products, dot_t(): lax.dot_general(a, b, (((1,), (1,)), ((), ())), preferred_element_type=f32)  48.6 us
    dot_general x25, matrix products, outer(): lax.dot_general(a, b, (((0,), (0,)), ((), ())), preferred_element_type=f32)  36.4 us
    dot_general x17, matrix products, dot(): return jnp.dot(a, b, preferred_element_type=f32)  31.9 us
    unnamed x660, local copies, waits for them, and re-layouts  28.1 us
    another operation x34, local copies, waits for them, and re-layouts, per_device(): jnp.stack(tap_terms, axis=1).reshape(heads, HEAD_DIM, TAPS)  23.3 us
    convert_element_type x1, other arithmetic, per_device(): back_values = (back_value_direct + conv_values).astype(bf16)  20.3 us
  transfers between devices with their start and end apart: 74, of which 26 were waited for; matrix products, arithmetic and copies ran while one was open for 57% of the time, Pallas kernels for 0%

profile of v1, /device:TPU:0, one launch (start us, length us, event | category | flops | bytes accessed | tf_op | source)
XLA Modules:
  0.0 714.3 jit_solution(16521496990743284267)
XLA Ops:
  9.8 3.0 collective-permute-start.1
  76.9 4.6 collective-permute-done.3
  83.9 5.6 collective-permute-done.4
  92.5 3.6 collective-permute-start.14
  97.1 4.7 collective-permute-start.6
  102.3 5.2 collective-permute-done.6
  108.5 3.0 fusion.421
  115.0 2.6 fusion.422
  141.8 3.2 fusion.423
  181.4 3.4 collective-permute-start.13
  185.5 3.7 collective-permute-done.13
  205.8 18.0 %fusion.90 = bf16[512,768]{0,1:T(8,128)(2,1)S(1)} fusion(f32[12,64,512]{2,1,0:T(8,128)S(1)} %fusion.201, f32[544,768]{0,1:T(8,128)S(1)} %fusion.118, f32[768]{0:T(1024)S(1)} %copy-done.195, f32[768]{0:T(1024)S(1)} %copy-done.197, f32[768]{0:T(1024)S(1)} %copy-done.199, f32[768]{0:T(1024)S(1)} %copy-done.201, f32[768]{0:T(1024)S(1)} %copy-done.203, ...), kind=kLoop, calls=%fused_computation.178 | loop fusion | flops 26345472 | bytes 54365184 | tf_op jit(solution)/shard_map/convert_element_type | solution.py:363
  230.7 2.5 multiply_convert_fusion.3
  244.6 2.6 fusion.427
  251.8 3.5 convert_reduce_fusion.6
  258.3 3.4 convert_reduce_fusion.3
  261.7 3.2 convert_reduce_fusion.4
  267.2 3.2 convert_reduce_fusion.5
  272.8 4.0 multiply_reduce_fusion
  278.7 8.2 %fusion.42 = (f32[768]{0:T(1024)}, f32[768]{0:T(1024)}, f32[768]{0:T(1024)}, f32[768]{0:T(1024)}, f32[768]{0:T(1024)}, /*index=5*/f32[768]{0:T(1024)}, f32[768]{...) fusion(f32[544,768]{0,1:T(8,128)S(1)} %fusion.118, ...), kind=kOutput, calls=%fused_computation.90 | convolution fusion | flops 616551168 | bytes 26391552 | tf_op jit(solution)/shard_map/dot_general | solution.py:33
  293.1 11.2 %fusion.43 = (f32[768]{0:T(1024)S(1)}, f32[768]{0:T(1024)}, f32[768]{0:T(1024)}, f32[768]{0:T(1024)}, f32[768]{0:T(1024)}, /*index=5*/f32[768]{0:T(1024)}, f32[7...) fusion(bf16[512,768]{0,1:T(8,128)(2,1)S(1)} %get-tuple-element., ...), kind=kLoop, calls=%fused_computation.91 | loop fusion | flops 14535168 | bytes 29153280 | tf_op jit(solution)/shard_map/reduce_sum | solution.py:412
  327.5 4.7 collective-permute-start.40
  367.0 2.6 collective-permute-done.29
  378.0 2.8 collective-permute-start.39
  427.9 20.3 %fusion.46 = bf16[512,768]{0,1:T(8,128)(2,1)S(1)} fusion(f32[544,768]{0,1:T(8,128)S(1)} %fusion.119, f32[12,64,512]{2,1,0:T(8,128)S(1)} %fusion.149, f32[768]{0:T(1024)S(1)} %copy-done.196, f32[768]{0:T(1024)S(1)} %copy-done.198, f32[768]{0:T(1024)S(1)} %copy-done.200, f32[768]{0:T(1024)S(1)} %copy-done.202, f32[768]{0:T(1024)S(1)} %copy-done.204, ...), kind=kLoop, calls=%fused_computation.95 | loop fusion | flops 26345472 | bytes 54365184 | tf_op jit(solution)/shard_map/convert_element_type | solution.py:451
  458.4 3.0 copy.680
  476.2 2.5 fusion.267
  478.8 2.5 fusion.270
  493.9 3.0 reshape_reshape.13
  546.5 2.8 collective-permute-done.53
  556.4 2.5 collective-permute-start.55
  558.9 3.4 collective-permute-done.55
  564.7 2.8 collective-permute-done.61
  577.2 3.3 add_convert_fusion.1
  581.1 3.1 add_convert_fusion
  587.5 2.5 gather_fusion.1
  593.9 2.5 gather_fusion.2
  597.0 6.2 select_convert_fusion
  603.2 2.8 copy.698
  605.9 6.7 copy.699
  617.5 40.9 %collective-permute-done.47 = bf16[768,576]{0,1:T(8,128)(2,1)} collective-permute-done((bf16[768,576]{0,1:T(8,128)(2,1)}, bf16[768,576]{0,1:T(8,128)(2,1)}, u32[]{:S(2)}, u32[]{:S(2)}) %collective-permute-start.47) | collective-permute-done | bytes 884768 | tf_op jit(solution)/shard_map/ppermute | solution.py:21
  658.4 3.0 convert_add_fusion.2
  661.4 2.9 copy.689
  670.0 9.8 %collective-permute-done.48 = bf16[4,96,576]{2,1,0:T(8,128)(2,1)S(1)} collective-permute-done((bf16[4,96,576]{2,1,0:T(8,128)(2,1)S(1)}, bf16[4,96,576]{2,1,0:T(8,128)(2,1)S(1)}, u32[]{:S(2)}, u32[]{:S(2)}) %collective-permute-start.48) | collective-permute-done | bytes 442400 | tf_op jit(solution)/shard_map/ppermute | solution.py:21
  683.3 7.7 %collective-permute-done.71 = bf16[4,96,768]{2,1,0:T(8,128)(2,1)S(1)} collective-permute-done((bf16[4,96,768]{2,1,0:T(8,128)(2,1)S(1)}, bf16[4,96,768]{2,1,0:T(8,128)(2,1)S(1)}, u32[]{:S(2)}, u32[]{:S(2)}) %collective-permute-start.71) | collective-permute-done | bytes 589856 | tf_op jit(solution)/shard_map/ppermute | solution.py:21
  693.7 4.4 collective-permute-done.50
  701.1 3.8 collective-permute-done.72
  705.1 5.6 collective-permute-done.67
  (1244 shorter events, 432.9 us)
Async XLA Ops:
  9.8 50.4 %collective-permute-start.1 = (bf16[784,384]{1,0:T(8,128)(2,1)}, bf16[784,384]{1,0:T(8,128)(2,1)}, u32[]{:S(2)}, u32[]{:S(2)}) collective-permute-start(bf16[784,384]{1,0:T(8,128)(2,1)} %pad_maximum_fusion.4), channel_id=1, source_target_pairs={{0,2},{1,3},{2,0},{3,1},{4,6},{5,7},{6,4},{7,5},{8,10},{9,11},{10,... | collective-permute-start | bytes 1806344 | tf_op jit(solution)/shard_map/ppermute | solution.py:21
  12.7 46.7 %collective-permute-start = (bf16[784,384]{1,0:T(8,128)(2,1)}, bf16[784,384]{1,0:T(8,128)(2,1)}, u32[]{:S(2)}, u32[]{:S(2)}) collective-permute-start(bf16[784,384]{1,0:T(8,128)(2,1)} %pad_maximum_fusion.4), channel_id=1, source_target_pairs={{0,1},{1,0},{2,3},{3,2},{4,5},{5,4},{6,7},{7,6},{8,9},{9,8},{10,11... | collective-permute-start | bytes 1806344 | tf_op jit(solution)/shard_map/ppermute | solution.py:21
  12.7 37.0 %collective-permute-start.8 = (bf16[768,192]{0,1:T(8,128)(2,1)}, bf16[768,192]{0,1:T(8,128)(2,1)}, u32[]{:S(2)}, u32[]{:S(2)}) collective-permute-start(bf16[768,192]{0,1:T(8,128)(2,1)} %param.25), channel_id=1, source_target_pairs={{0,2},{1,3},{2,0},{3,1},{4,6},{5,7},{6,4},{7,5},{8,10},{9,11},{10,... | collective-permute-start | bytes 884744 | tf_op jit(solution)/shard_map/ppermute | solution.py:21
  12.8 39.3 %collective-permute-start.7 = (bf16[768,192]{0,1:T(8,128)(2,1)}, bf16[768,192]{0,1:T(8,128)(2,1)}, u32[]{:S(2)}, u32[]{:S(2)}) collective-permute-start(bf16[768,192]{0,1:T(8,128)(2,1)} %param.25), channel_id=1, source_target_pairs={{0,1},{1,0},{2,3},{3,2},{4,5},{5,4},{6,7},{7,6},{8,9},{9,8},{10,11... | collective-permute-start | bytes 884744 | tf_op jit(solution)/shard_map/ppermute | solution.py:21
  13.3 39.1 %collective-permute-start.17 = (bf16[192,768]{1,0:T(8,128)(2,1)}, bf16[192,768]{1,0:T(8,128)(2,1)}, u32[]{:S(2)}, u32[]{:S(2)}) collective-permute-start(bf16[192,768]{1,0:T(8,128)(2,1)} %param.28), channel_id=1, source_target_pairs={{0,2},{1,3},{2,0},{3,1},{4,6},{5,7},{6,4},{7,5},{8,10},{9,11},{10,... | collective-permute-start | bytes 884744 | tf_op jit(solution)/shard_map/ppermute | solution.py:21
  52.1 118.6 %collective-permute-start.21 = (bf16[768,768]{1,0:T(8,128)(2,1)}, bf16[768,768]{1,0:T(8,128)(2,1)}, u32[]{:S(2)}, u32[]{:S(2)}) collective-permute-start(bf16[768,768]{1,0:T(8,128)(2,1)} %param.32), channel_id=1, source_target_pairs={{0,2},{1,3},{2,0},{3,1},{4,6},{5,7},{6,4},{7,5},{8,10},{9,11},{10,... | collective-permute-start | bytes 3538952 | tf_op jit(solution)/shard_map/ppermute | solution.py:21
  56.0 181.8 %collective-permute-start.19 = (bf16[768,768]{1,0:T(8,128)(2,1)}, bf16[768,768]{1,0:T(8,128)(2,1)}, u32[]{:S(2)}, u32[]{:S(2)}) collective-permute-start(bf16[768,768]{1,0:T(8,128)(2,1)} %param.32), channel_id=1, source_target_pairs={{0,1},{1,0},{2,3},{3,2},{4,5},{5,4},{6,7},{7,6},{8,9},{9,8},{10,11... | collective-permute-start | bytes 3538952 | tf_op jit(solution)/shard_map/ppermute | solution.py:21
  56.5 114.2 %collective-permute-start.22 = (bf16[768,768]{1,0:T(8,128)(2,1)}, bf16[768,768]{1,0:T(8,128)(2,1)}, u32[]{:S(2)}, u32[]{:S(2)}) collective-permute-start(bf16[768,768]{1,0:T(8,128)(2,1)} %param.34), channel_id=1, source_target_pairs={{0,2},{1,3},{2,0},{3,1},{4,6},{5,7},{6,4},{7,5},{8,10},{9,11},{10,... | collective-permute-start | bytes 3538952 | tf_op jit(solution)/shard_map/ppermute | solution.py:21
  83.3 9.2 %collective-permute-start.5 = (bf16[64,1536]{1,0:T(8,128)(2,1)S(1)}, bf16[64,1536]{1,0:T(8,128)(2,1)S(1)}, u32[]{:S(2)}, u32[]{:S(2)}) collective-permute-start(bf16[64,1536]{1,0:T(8,128)(2,1)S(1)} %get-tuple-element.302), channel_id=1, source_target_pairs={{0,8},{4,12},{8,0},{12,4},{16,24},{20,28},{24,16},{28,20},{1,9},{5... | collective-permute-start | bytes 589832 | tf_op jit(solution)/shard_map/ppermute | solution.py:21
  92.5 9.3 %collective-permute-start.14 = (bf16[16,768]{0,1:T(8,128)(2,1)S(1)}, bf16[16,768]{0,1:T(8,128)(2,1)S(1)}, u32[]{:S(2)}, u32[]{:S(2)}) collective-permute-start(bf16[16,768]{0,1:T(8,128)(2,1)S(1)} %get-tuple-element.292), channel_id=1, source_target_pairs={{0,4},{4,8},{8,12},{12,16},{16,20},{20,24},{24,28},{1,5},{5,9},{9,... | collective-permute-start | bytes 73736 | tf_op jit(solution)/shard_map/ppermute | solution.py:311
  97.1 10.4 %collective-permute-start.6 = (bf16[64,1536]{1,0:T(8,128)(2,1)S(1)}, bf16[64,1536]{1,0:T(8,128)(2,1)S(1)}, u32[]{:S(2)}, u32[]{:S(2)}) collective-permute-start(bf16[64,1536]{1,0:T(8,128)(2,1)S(1)} %select_convert_fusion.1), channel_id=1, source_target_pairs={{0,16},{4,20},{8,24},{12,28},{16,0},{20,4},{24,8},{28,12},{1,17},{... | collective-permute-start | bytes 589832 | tf_op jit(solution)/shard_map/ppermute | solution.py:21
  120.3 26.3 %collective-permute-start.10 = (bf16[64,896]{1,0:T(8,128)(2,1)}, bf16[64,896]{1,0:T(8,128)(2,1)}, u32[]{:S(2)}, u32[]{:S(2)}) collective-permute-start(bf16[64,896]{1,0:T(8,128)(2,1)} %concatenate.156), channel_id=1, source_target_pairs={{0,4},{4,0},{8,12},{12,8},{16,20},{20,16},{24,28},{28,24},{1,5},{5... | collective-permute-start | bytes 344072 | tf_op jit(solution)/shard_map/ppermute | solution.py:21
  170.6 69.4 %collective-permute-start.20 = (bf16[768,768]{1,0:T(8,128)(2,1)}, bf16[768,768]{1,0:T(8,128)(2,1)}, u32[]{:S(2)}, u32[]{:S(2)}) collective-permute-start(bf16[768,768]{1,0:T(8,128)(2,1)} %param.34), channel_id=1, source_target_pairs={{0,1},{1,0},{2,3},{3,2},{4,5},{5,4},{6,7},{7,6},{8,9},{9,8},{10,11... | collective-permute-start | bytes 3538952 | tf_op jit(solution)/shard_map/ppermute | solution.py:21
  170.7 71.8 %collective-permute-start.23 = (bf16[768,768]{1,0:T(8,128)(2,1)}, bf16[768,768]{1,0:T(8,128)(2,1)}, u32[]{:S(2)}, u32[]{:S(2)}) collective-permute-start(bf16[768,768]{1,0:T(8,128)(2,1)} %collective-permute-done.21), channel_id=1, source_target_pairs={{0,1},{1,0},{2,3},{3,2},{4,5},{5,4},{6,7},{7,6},{8,9},{9,8},{10,11... | collective-permute-start | bytes 3538952 | tf_op jit(solution)/shard_map/ppermute | solution.py:21
  171.2 73.4 %collective-permute-start.24 = (bf16[768,768]{1,0:T(8,128)(2,1)}, bf16[768,768]{1,0:T(8,128)(2,1)}, u32[]{:S(2)}, u32[]{:S(2)}) collective-permute-start(bf16[768,768]{1,0:T(8,128)(2,1)} %collective-permute-done.22), channel_id=1, source_target_pairs={{0,1},{1,0},{2,3},{3,2},{4,5},{5,4},{6,7},{7,6},{8,9},{9,8},{10,11... | collective-permute-start | bytes 3538952 | tf_op jit(solution)/shard_map/ppermute | solution.py:21
  320.7 42.1 %collective-permute-start.28 = (bf16[64,768]{1,0:T(8,128)(2,1)}, bf16[64,768]{1,0:T(8,128)(2,1)}, u32[]{:S(2)}, u32[]{:S(2)}) collective-permute-start(bf16[64,768]{1,0:T(8,128)(2,1)} %convert_element_type.649), channel_id=1, source_target_pairs={{0,4},{4,0},{8,12},{12,8},{16,20},{20,16},{24,28},{28,24},{1,5},{5... | collective-permute-start | bytes 294920 | tf_op jit(solution)/shard_map/ppermute | solution.py:21
  322.8 41.7 %collective-permute-start.36 = (bf16[64,768]{1,0:T(8,128)(2,1)}, bf16[64,768]{1,0:T(8,128)(2,1)}, u32[]{:S(2)}, u32[]{:S(2)}) collective-permute-start(bf16[64,768]{1,0:T(8,128)(2,1)} %convert_element_type.670), channel_id=1, source_target_pairs={{0,4},{4,0},{8,12},{12,8},{16,20},{20,16},{24,28},{28,24},{1,5},{5... | collective-permute-start | bytes 294920 | tf_op jit(solution)/shard_map/ppermute | solution.py:21
  326.2 33.5 %collective-permute-start.41 = (bf16[16,768]{0,1:T(8,128)(2,1)}, bf16[16,768]{0,1:T(8,128)(2,1)S(1)}, u32[]{:S(2)}, u32[]{:S(2)}) collective-permute-start(bf16[16,768]{0,1:T(8,128)(2,1)} %get-tuple-element.291), channel_id=1, source_target_pairs={{4,0},{8,4},{12,8},{16,12},{20,16},{24,20},{28,24},{5,1},{9,5},{13... | collective-permute-start | bytes 73736 | tf_op jit(solution)/shard_map/ppermute | solution.py:312
  327.5 32.2 %collective-permute-start.40 = (bf16[16,768]{0,1:T(8,128)(2,1)S(1)}, bf16[16,768]{0,1:T(8,128)(2,1)S(1)}, u32[]{:S(2)}, u32[]{:S(2)}) collective-permute-start(bf16[16,768]{0,1:T(8,128)(2,1)S(1)} %copy-done.174), channel_id=1, source_target_pairs={{0,4},{4,8},{8,12},{12,16},{16,20},{20,24},{24,28},{1,5},{5,9},{9,... | collective-permute-start | bytes 73736 | tf_op jit(solution)/shard_map/ppermute | solution.py:311
  332.3 243.8 %collective-permute-start.26 = (bf16[512,768]{0,1:T(8,128)(2,1)}, bf16[512,768]{0,1:T(8,128)(2,1)}, u32[]{:S(2)}, u32[]{:S(2)}) collective-permute-start(bf16[512,768]{0,1:T(8,128)(2,1)} %get-tuple-element.281), channel_id=1, source_target_pairs={{0,2},{1,3},{2,0},{3,1},{4,6},{5,7},{6,4},{7,5},{8,10},{9,11},{10,... | collective-permute-start | bytes 2359304 | tf_op jit(solution)/shard_map/ppermute | solution.py:21
  359.7 21.1 %collective-permute-start.57 = (bf16[768,192]{0,1:T(8,128)(2,1)}, bf16[768,192]{0,1:T(8,128)(2,1)S(1)}, u32[]{:S(2)}, u32[]{:S(2)}) collective-permute-start(bf16[768,192]{0,1:T(8,128)(2,1)} %convolution_convert_fusion.13), channel_id=1, source_target_pairs={{0,1},{1,0},{2,3},{3,2},{4,5},{5,4},{6,7},{7,6},{8,9},{9,8},{10,11... | collective-permute-start | bytes 884744 | tf_op jit(solution)/shard_map/ppermute | solution.py:21
  361.0 129.6 %collective-permute-start.56 = (bf16[768,192]{0,1:T(8,128)(2,1)}, bf16[768,192]{0,1:T(8,128)(2,1)}, u32[]{:S(2)}, u32[]{:S(2)}) collective-permute-start(bf16[768,192]{0,1:T(8,128)(2,1)} %convolution_convert_fusion.15), channel_id=1, source_target_pairs={{0,1},{1,0},{2,3},{3,2},{4,5},{5,4},{6,7},{7,6},{8,9},{9,8},{10,11... | collective-permute-start | bytes 884744 | tf_op jit(solution)/shard_map/ppermute | solution.py:21
  374.9 9.5 %collective-permute-start.31 = (bf16[64,768]{1,0:T(8,128)(2,1)S(1)}, bf16[64,768]{1,0:T(8,128)(2,1)S(1)}, u32[]{:S(2)}, u32[]{:S(2)}) collective-permute-start(bf16[64,768]{1,0:T(8,128)(2,1)S(1)} %select_convert_fusion.4), channel_id=1, source_target_pairs={{0,16},{4,20},{8,24},{12,28},{16,0},{20,4},{24,8},{28,12},{1,17},{... | collective-permute-start | bytes 294920 | tf_op jit(solution)/shard_map/ppermute | solution.py:21
  378.0 83.8 %collective-permute-start.39 = (bf16[64,768]{1,0:T(8,128)(2,1)}, bf16[64,768]{1,0:T(8,128)(2,1)}, u32[]{:S(2)}, u32[]{:S(2)}) collective-permute-start(bf16[64,768]{1,0:T(8,128)(2,1)} %select_convert_fusion.2), channel_id=1, source_target_pairs={{0,16},{4,20},{8,24},{12,28},{16,0},{20,4},{24,8},{28,12},{1,17},{... | collective-permute-start | bytes 294920 | tf_op jit(solution)/shard_map/ppermute | solution.py:21
  382.9 108.8 %collective-permute-start.58 = (bf16[768,192]{0,1:T(8,128)(2,1)}, bf16[768,192]{0,1:T(8,128)(2,1)}, u32[]{:S(2)}, u32[]{:S(2)}) collective-permute-start(bf16[768,192]{0,1:T(8,128)(2,1)} %add_convert_fusion.11), channel_id=1, source_target_pairs={{0,2},{1,3},{2,0},{3,1},{4,6},{5,7},{6,4},{7,5},{8,10},{9,11},{10,... | collective-permute-start | bytes 884744 | tf_op jit(solution)/shard_map/ppermute | solution.py:21
  488.5 88.2 %collective-permute-start.63 = (bf16[768,768]{1,0:T(8,128)(2,1)}, bf16[768,768]{1,0:T(8,128)(2,1)}, u32[]{:S(2)}, u32[]{:S(2)}) collective-permute-start(bf16[768,768]{1,0:T(8,128)(2,1)} %convolution_convert_fusion.4), channel_id=1, source_target_pairs={{0,1},{1,0},{2,3},{3,2},{4,5},{5,4},{6,7},{7,6},{8,9},{9,8},{10,11... | collective-permute-start | bytes 3538952 | tf_op jit(solution)/shard_map/ppermute | solution.py:21
  488.7 88.1 %collective-permute-start.69 = (bf16[768,768]{1,0:T(8,128)(2,1)}, bf16[768,768]{1,0:T(8,128)(2,1)}, u32[]{:S(2)}, u32[]{:S(2)}) collective-permute-start(bf16[768,768]{1,0:T(8,128)(2,1)} %convolution_convert_fusion), channel_id=1, source_target_pairs={{0,1},{1,0},{2,3},{3,2},{4,5},{5,4},{6,7},{7,6},{8,9},{9,8},{10,11... | collective-permute-start | bytes 3538952 | tf_op jit(solution)/shard_map/ppermute | solution.py:21
  490.6 15.3 %collective-permute-start.35 = (bf16[64,768]{1,0:T(8,128)(2,1)}, bf16[64,768]{1,0:T(8,128)(2,1)}, u32[]{:S(2)}, u32[]{:S(2)}) collective-permute-start(bf16[64,768]{1,0:T(8,128)(2,1)} %select_convert_fusion.3), channel_id=1, source_target_pairs={{0,16},{4,20},{8,24},{12,28},{16,0},{20,4},{24,8},{28,12},{1,17},{... | collective-permute-start | bytes 294920 | tf_op jit(solution)/shard_map/ppermute | solution.py:21
  505.0 45.6 %collective-permute-start.59 = (bf16[4,96,192]{2,1,0:T(8,128)(2,1)}, bf16[4,96,192]{2,1,0:T(8,128)(2,1)}, u32[]{:S(2)}, u32[]{:S(2)}) collective-permute-start(bf16[4,96,192]{2,1,0:T(8,128)(2,1)} %bitcast.555), channel_id=1, source_target_pairs={{0,4},{4,0},{8,12},{12,8},{16,20},{20,16},{24,28},{28,24},{1,5},{5... | collective-permute-start | bytes 442376 | tf_op jit(solution)/shard_map/ppermute | solution.py:21
  530.6 10.5 %collective-permute-start.51 = (f32[80,128]{1,0:T(8,128)S(1)}, f32[80,128]{1,0:T(8,128)S(1)}, u32[]{:S(2)}, u32[]{:S(2)}) collective-permute-start(f32[80,128]{1,0:T(8,128)S(1)} %pad_bitcast_fusion), channel_id=1, source_target_pairs={{0,1},{1,0},{2,3},{3,2},{4,5},{5,4},{6,7},{7,6},{8,9},{9,8},{10,11... | collective-permute-start | bytes 122888 | tf_op jit(solution)/shard_map/ppermute | solution.py:21
  553.7 26.8 %collective-permute-start.43 = (bf16[512,768]{0,1:T(8,128)(2,1)}, bf16[512,768]{0,1:T(8,128)(2,1)}, u32[]{:S(2)}, u32[]{:S(2)}) collective-permute-start(bf16[512,768]{0,1:T(8,128)(2,1)} %add_convert_fusion.3), channel_id=1, source_target_pairs={{0,2},{1,3},{2,0},{3,1},{4,6},{5,7},{6,4},{7,5},{8,10},{9,11},{10,... | collective-permute-start | bytes 2359304 | tf_op jit(solution)/shard_map/ppermute | solution.py:21
  567.5 13.2 %collective-permute-start.46 = (bf16[768,576]{0,1:T(8,128)(2,1)S(1)}, bf16[768,576]{0,1:T(8,128)(2,1)S(1)}, u32[]{:S(2)}, u32[]{:S(2)}) collective-permute-start(bf16[768,576]{0,1:T(8,128)(2,1)S(1)} %pad_maximum_fusion.3), channel_id=1, source_target_pairs={{0,1},{1,0},{2,3},{3,2},{4,5},{5,4},{6,7},{7,6},{8,9},{9,8},{10,11... | collective-permute-start | bytes 2654216 | tf_op jit(solution)/shard_map/ppermute | solution.py:21
  576.1 9.3 %collective-permute-start.25 = (bf16[512,768]{0,1:T(8,128)(2,1)S(1)}, bf16[512,768]{0,1:T(8,128)(2,1)S(1)}, u32[]{:S(2)}, u32[]{:S(2)}) collective-permute-start(bf16[512,768]{0,1:T(8,128)(2,1)S(1)} %copy-done.88), channel_id=1, source_target_pairs={{0,1},{1,0},{2,3},{3,2},{4,5},{5,4},{6,7},{7,6},{8,9},{9,8},{10,11... | collective-permute-start | bytes 2359304 | tf_op jit(solution)/shard_map/ppermute | solution.py:21
  576.7 19.8 %collective-permute-start.62 = (bf16[768,768]{1,0:T(8,128)(2,1)}, bf16[768,768]{1,0:T(8,128)(2,1)}, u32[]{:S(2)}, u32[]{:S(2)}) collective-permute-start(bf16[768,768]{1,0:T(8,128)(2,1)} %convolution_convert_fusion.6), channel_id=1, source_target_pairs={{0,1},{1,0},{2,3},{3,2},{4,5},{5,4},{6,7},{7,6},{8,9},{9,8},{10,11... | collective-permute-start | bytes 3538952 | tf_op jit(solution)/shard_map/ppermute | solution.py:21
  580.5 9.5 %collective-permute-start.42 = (bf16[512,768]{0,1:T(8,128)(2,1)}, bf16[512,768]{0,1:T(8,128)(2,1)}, u32[]{:S(2)}, u32[]{:S(2)}) collective-permute-start(bf16[512,768]{0,1:T(8,128)(2,1)} %add_convert_fusion.3), channel_id=1, source_target_pairs={{0,1},{1,0},{2,3},{3,2},{4,5},{5,4},{6,7},{7,6},{8,9},{9,8},{10,11... | collective-permute-start | bytes 2359304 | tf_op jit(solution)/shard_map/ppermute | solution.py:21
  580.7 9.5 %collective-permute-start.44 = (bf16[512,768]{0,1:T(8,128)(2,1)}, bf16[512,768]{0,1:T(8,128)(2,1)}, u32[]{:S(2)}, u32[]{:S(2)}) collective-permute-start(bf16[512,768]{0,1:T(8,128)(2,1)} %collective-permute-done.43), channel_id=1, source_target_pairs={{0,1},{1,0},{2,3},{3,2},{4,5},{5,4},{6,7},{7,6},{8,9},{9,8},{10,11... | collective-permute-start | bytes 2359304 | tf_op jit(solution)/shard_map/ppermute | solution.py:21
  585.4 80.3 %collective-permute-start.68 = (bf16[768,768]{1,0:T(8,128)(2,1)}, bf16[768,768]{1,0:T(8,128)(2,1)}, u32[]{:S(2)}, u32[]{:S(2)}) collective-permute-start(bf16[768,768]{1,0:T(8,128)(2,1)} %convolution_convert_fusion.2), channel_id=1, source_target_pairs={{0,1},{1,0},{2,3},{3,2},{4,5},{5,4},{6,7},{7,6},{8,9},{9,8},{10,11... | collective-permute-start | bytes 3538952 | tf_op jit(solution)/shard_map/ppermute | solution.py:21
  585.5 29.1 %collective-permute-start.64 = (bf16[768,768]{1,0:T(8,128)(2,1)}, bf16[768,768]{1,0:T(8,128)(2,1)}, u32[]{:S(2)}, u32[]{:S(2)}) collective-permute-start(bf16[768,768]{1,0:T(8,128)(2,1)} %add_convert_fusion.1), channel_id=1, source_target_pairs={{0,2},{1,3},{2,0},{3,1},{4,6},{5,7},{6,4},{7,5},{8,10},{9,11},{10,... | collective-permute-start | bytes 3538952 | tf_op jit(solution)/shard_map/ppermute | solution.py:21
  590.0 27.5 %collective-permute-start.45 = (bf16[768,576]{0,1:T(8,128)(2,1)}, bf16[768,576]{0,1:T(8,128)(2,1)}, u32[]{:S(2)}, u32[]{:S(2)}) collective-permute-start(bf16[768,576]{0,1:T(8,128)(2,1)} %pad_maximum_fusion.2), channel_id=1, source_target_pairs={{0,1},{1,0},{2,3},{3,2},{4,5},{5,4},{6,7},{7,6},{8,9},{9,8},{10,11... | collective-permute-start | bytes 2654216 | tf_op jit(solution)/shard_map/ppermute | solution.py:21
  590.2 75.5 %collective-permute-start.70 = (bf16[768,768]{1,0:T(8,128)(2,1)}, bf16[768,768]{1,0:T(8,128)(2,1)}, u32[]{:S(2)}, u32[]{:S(2)}) collective-permute-start(bf16[768,768]{1,0:T(8,128)(2,1)} %add_convert_fusion), channel_id=1, source_target_pairs={{0,2},{1,3},{2,0},{3,1},{4,6},{5,7},{6,4},{7,5},{8,10},{9,11},{10,... | collective-permute-start | bytes 3538952 | tf_op jit(solution)/shard_map/ppermute | solution.py:21
  596.5 61.9 %collective-permute-start.47 = (bf16[768,576]{0,1:T(8,128)(2,1)}, bf16[768,576]{0,1:T(8,128)(2,1)}, u32[]{:S(2)}, u32[]{:S(2)}) collective-permute-start(bf16[768,576]{0,1:T(8,128)(2,1)} %add_convert_fusion.2), channel_id=1, source_target_pairs={{0,2},{1,3},{2,0},{3,1},{4,6},{5,7},{6,4},{7,5},{8,10},{9,11},{10,... | collective-permute-start | bytes 2654216 | tf_op jit(solution)/shard_map/ppermute | solution.py:21
  617.5 62.5 %collective-permute-start.65 = (bf16[4,96,768]{2,1,0:T(8,128)(2,1)}, bf16[4,96,768]{2,1,0:T(8,128)(2,1)}, u32[]{:S(2)}, u32[]{:S(2)}) collective-permute-start(bf16[4,96,768]{2,1,0:T(8,128)(2,1)} %fusion.152), channel_id=1, source_target_pairs={{0,4},{4,0},{8,12},{12,8},{16,20},{20,16},{24,28},{28,24},{1,5},{5... | collective-permute-start | bytes 1769480 | tf_op jit(solution)/shard_map/ppermute | solution.py:21
  665.6 14.2 %collective-permute-start.48 = (bf16[4,96,576]{2,1,0:T(8,128)(2,1)S(1)}, bf16[4,96,576]{2,1,0:T(8,128)(2,1)S(1)}, u32[]{:S(2)}, u32[]{:S(2)}) collective-permute-start(bf16[4,96,576]{2,1,0:T(8,128)(2,1)S(1)} %fusion.175), channel_id=1, source_target_pairs={{0,4},{4,0},{8,12},{12,8},{16,20},{20,16},{24,28},{28,24},{1,5},{5... | collective-permute-start | bytes 1327112 | tf_op jit(solution)/shard_map/ppermute | solution.py:21
  667.9 23.1 %collective-permute-start.71 = (bf16[4,96,768]{2,1,0:T(8,128)(2,1)S(1)}, bf16[4,96,768]{2,1,0:T(8,128)(2,1)S(1)}, u32[]{:S(2)}, u32[]{:S(2)}) collective-permute-start(bf16[4,96,768]{2,1,0:T(8,128)(2,1)S(1)} %fusion.153), channel_id=1, source_target_pairs={{0,4},{4,0},{8,12},{12,8},{16,20},{20,16},{24,28},{28,24},{1,5},{5... | collective-permute-start | bytes 1769480 | tf_op jit(solution)/shard_map/ppermute | solution.py:21
  679.9 11.3 %collective-permute-start.49 = (bf16[2,96,576]{2,1,0:T(8,128)(2,1)S(1)}, bf16[2,96,576]{2,1,0:T(8,128)(2,1)S(1)}, u32[]{:S(2)}, u32[]{:S(2)}) collective-permute-start(bf16[2,96,576]{2,1,0:T(8,128)(2,1)S(1)} %fusion.212), channel_id=1, source_target_pairs={{0,8},{4,12},{8,0},{12,4},{16,24},{20,28},{24,16},{28,20},{1,9},{5... | collective-permute-start | bytes 663560 | tf_op jit(solution)/shard_map/ppermute | solution.py:21
  681.3 17.7 %collective-permute-start.66 = (bf16[2,96,768]{2,1,0:T(8,128)(2,1)S(1)}, bf16[2,96,768]{2,1,0:T(8,128)(2,1)S(1)}, u32[]{:S(2)}, u32[]{:S(2)}) collective-permute-start(bf16[2,96,768]{2,1,0:T(8,128)(2,1)S(1)} %fusion.207), channel_id=1, source_target_pairs={{0,8},{4,12},{8,0},{12,4},{16,24},{20,28},{24,16},{28,20},{1,9},{5... | collective-permute-start | bytes 884744 | tf_op jit(solution)/shard_map/ppermute | solution.py:21
  693.0 11.9 %collective-permute-start.72 = (bf16[2,96,768]{2,1,0:T(8,128)(2,1)S(1)}, bf16[2,96,768]{2,1,0:T(8,128)(2,1)S(1)}, u32[]{:S(2)}, u32[]{:S(2)}) collective-permute-start(bf16[2,96,768]{2,1,0:T(8,128)(2,1)S(1)} %fusion.208), channel_id=1, source_target_pairs={{0,8},{4,12},{8,0},{12,4},{16,24},{20,28},{24,16},{28,20},{1,9},{5... | collective-permute-start | bytes 884744 | tf_op jit(solution)/shard_map/ppermute | solution.py:21
  699.0 11.6 %collective-permute-start.67 = (bf16[1,96,768]{2,1,0:T(8,128)(2,1)S(1)}, bf16[1,96,768]{2,1,0:T(8,128)(2,1)S(1)}, u32[]{:S(2)}, u32[]{:S(2)}) collective-permute-start(bf16[1,96,768]{2,1,0:T(8,128)(2,1)S(1)} %dynamic-slice_convert_fusion.5), channel_id=1, source_target_pairs={{0,16},{4,20},{8,24},{12,28},{16,0},{20,4},{24,8},{28,12},{1,17},{... | collective-permute-start | bytes 442376 | tf_op jit(solution)/shard_map/ppermute | solution.py:21
  (335 other events, 2418.7 us)
